TPU v7x, 32 devices: a whole 2x2x4 slice. The times are simulated.
32 devices in a mesh: ctx: 8 (over z, y), fsdp: 4 (over x, core).
Axes of the slice: x: 2, y: 2, z: 4, core: 2. Of those that a mesh axis runs over, the one named last changes fastest.
Arguments:
- tokens: bfloat16 [4, 2048, 768], P('fsdp', 'ctx'), may hold values from -6 to 6
- pair_order: int32 [8], replicated, may hold values from 0 to 7, each once
- norm_one: bfloat16 [768], P('fsdp'), may hold values from 0.099609375 to 1.8984375
- qkv_weight: bfloat16 [768, 2304], P('fsdp'), may hold values from -0.3125 to 0.3125
- out_weight: bfloat16 [768, 768], P('fsdp'), may hold values from -1.75 to 1.75
- norm_two: bfloat16 [768], P('fsdp'), may hold values from 0.099609375 to 1.8984375
- gateup_weight: bfloat16 [768, 2304], P('fsdp'), may hold values from -0.21875 to 0.21875
- down_weight: bfloat16 [1152, 768], P('fsdp'), may hold values from -0.1875 to 0.1875
- cotangent: bfloat16 [4, 2048, 768], P('fsdp', 'ctx'), may hold values from -6 to 6
Outputs:
- layer_out: bfloat16 [4, 2048, 768], P('fsdp', 'ctx')
- grad_tokens: float32 [4, 2048, 768], P('fsdp', 'ctx')
- grad_norm_one: float32 [768], P('fsdp')
- grad_qkv_weight: float32 [768, 2304], P('fsdp')
- grad_out_weight: float32 [768, 768], P('fsdp')
- grad_norm_two: float32 [768], P('fsdp')
- grad_gateup_weight: float32 [768, 2304], P('fsdp')
- grad_down_weight: float32 [1152, 768], P('fsdp')
Inputs may be any that keep to these rules, and one draw needn't show every extreme that they name: Device j of ctx holds position block pair_order[j] of its sequence in its first 128 slots and block 15 - pair_order[j] in its last 128 slots; every block once.
All inputs are finite; a program needn't handle non-finite values.
Results may differ from a plain program's by a relative error of at most 0.018.
The roundings to bfloat16 on the way count: a program that leaves them out, or rounds other values in their place, can miss the bound.
Values may be sent and summed in bfloat16 or wider, within the bound.
No kernel may reach another device: no remote copies, remote signals or barrier semaphores. Data moves between devices by JAX's collectives and lax.ppermute only.
A program may use at most 320 MiB of HBM per device.

v0:
```python
from functools import partial

import jax
import jax.numpy as jnp
from jax import lax
from jax.sharding import PartitionSpec as P

D = 768
HEADS = 12
HEAD_DIM = 64
FF = 1152
KEYBLK = 512


theta_base = 160000.0
norm_eps = 1e-05
neg_large = -1e30


def layer_norm(token_rows, gain_row):
    mean_value = jnp.mean(token_rows, axis=-1, keepdims=True)
    centered = token_rows - mean_value
    spread = jnp.mean(centered * centered, axis=-1, keepdims=True)
    return centered * lax.rsqrt(spread + norm_eps) * gain_row


def rotate(token_rows, positions):
    row_count = token_rows.shape[0]
    half_dim = HEAD_DIM // 2
    frequency = theta_base ** (-2.0 * jnp.arange(half_dim, dtype=jnp.float32) / HEAD_DIM)
    angles = positions.astype(jnp.float32)[:, None] * frequency[None, :]
    cosine = jnp.concatenate([jnp.cos(angles), jnp.cos(angles)], axis=1)[:, None, :]
    sine_table = jnp.concatenate([jnp.sin(angles), jnp.sin(angles)], axis=1)[:, None, :]
    by_heads = token_rows.reshape(row_count, HEADS, HEAD_DIM)
    turned = jnp.concatenate([-by_heads[..., half_dim:], by_heads[..., :half_dim]], axis=-1)
    return (by_heads * cosine + turned * sine_table).reshape(row_count, HEADS * HEAD_DIM)


def geglu(gate_part, up_part):
    return jax.nn.gelu(gate_part, approximate=False) * up_part


def lookup(lookup_table, wanted):
    slot_ids = jnp.arange(lookup_table.shape[0], dtype=jnp.int32)
    picked = jnp.where(slot_ids[None, :] == wanted[:, None], lookup_table[None, :], 0)
    return jnp.sum(picked, axis=1)


def block_source(pair_order, ctx_count):
    block_ids = jnp.arange(2 * ctx_count, dtype=jnp.int32)
    mirror = jnp.where(block_ids < ctx_count, block_ids, 2 * ctx_count - 1 - block_ids)
    device_ids = jnp.arange(ctx_count, dtype=jnp.int32)
    owner = jnp.sum(
        jnp.where(pair_order[None, :] == mirror[:, None], device_ids[None, :], 0), axis=1
    )
    return 2 * owner + (block_ids >= ctx_count).astype(jnp.int32)


def block_target(pair_order, ctx_count):
    block_ids = jnp.arange(2 * ctx_count, dtype=jnp.int32)
    first_block = lookup(pair_order, block_ids // 2)
    return jnp.where(block_ids % 2 == 0, first_block, 2 * ctx_count - 1 - first_block)


def reorder(block_rows, order_index, block_width):
    grouped = block_rows.reshape((order_index.shape[0], block_width) + block_rows.shape[1:])
    return jnp.take(grouped, order_index, axis=0).reshape(block_rows.shape)


def masked_scores(query_heads, query_pos, key_heads, key_first):
    raw_scores = jnp.einsum(
        "qhd,khd->hqk", query_heads, key_heads, preferred_element_type=jnp.float32
    ) * HEAD_DIM ** (-0.5)
    key_pos = key_first + jnp.arange(key_heads.shape[0], dtype=jnp.int32)
    return jnp.where(key_pos[None, None, :] <= query_pos[None, :, None], raw_scores, neg_large)


def block_count(position_block, block_width):
    return ((position_block + 1) * block_width + KEYBLK - 1) // KEYBLK


def forward_rows(query_heads, query_pos, key_rows, value_rows, count_blocks):
    row_count = query_heads.shape[0]

    def first_pass(block_index, partial_state):
        row_top, row_total = partial_state
        first_key = block_index * KEYBLK
        key_block = lax.dynamic_slice_in_dim(key_rows, first_key, KEYBLK, 0)
        scores = masked_scores(query_heads, query_pos, key_block, first_key)
        new_top = jnp.maximum(row_top, jnp.max(scores, axis=-1))
        row_total = row_total * jnp.exp(row_top - new_top) + jnp.sum(
            jnp.exp(scores - new_top[:, :, None]), axis=-1
        )
        return (new_top, row_total)

    start_top = jnp.full((HEADS, row_count), neg_large, jnp.float32)
    start_total = jnp.zeros((HEADS, row_count), jnp.float32)
    row_top, row_total = lax.fori_loop(0, count_blocks, first_pass, (start_top, start_total))
    log_total = row_top + jnp.log(row_total)

    def second_pass(block_index, partial_state):
        attended, fine_part = partial_state
        first_key = block_index * KEYBLK
        key_block = lax.dynamic_slice_in_dim(key_rows, first_key, KEYBLK, 0)
        value_block = lax.dynamic_slice_in_dim(value_rows, first_key, KEYBLK, 0)
        probability = jnp.exp(
            masked_scores(query_heads, query_pos, key_block, first_key) - log_total[:, :, None]
        )
        coarse = probability.astype(jnp.bfloat16)
        remainder = (probability - coarse.astype(jnp.float32)).astype(jnp.bfloat16)
        attended = attended + jnp.einsum(
            "hqk,khd->qhd", coarse, value_block, preferred_element_type=jnp.float32
        )
        fine_part = fine_part + jnp.einsum(
            "hqk,khd->qhd", remainder, value_block, preferred_element_type=jnp.float32
        )
        return (attended, fine_part)

    zero_heads = jnp.zeros(query_heads.shape, jnp.float32)
    attended, fine_part = lax.fori_loop(0, count_blocks, second_pass, (zero_heads, zero_heads))
    return (attended, attended + fine_part, log_total)


def backward_rows(
    query_heads,
    query_pos,
    grad_heads,
    log_total,
    row_delta,
    key_rows,
    value_rows,
    count_blocks,
    keys_sum,
    values_sum,
):

    def advance(block_index, partial_state):
        grad_query, keys_acc, values_acc = partial_state
        first_key = block_index * KEYBLK
        key_block = lax.dynamic_slice_in_dim(key_rows, first_key, KEYBLK, 0)
        value_block = lax.dynamic_slice_in_dim(value_rows, first_key, KEYBLK, 0)
        probability = jnp.exp(
            masked_scores(query_heads, query_pos, key_block, first_key) - log_total[:, :, None]
        )
        grad_prob = jnp.einsum(
            "qhd,khd->hqk", grad_heads, value_block, preferred_element_type=jnp.float32
        )
        grad_scores = (probability * (grad_prob - row_delta[:, :, None])).astype(jnp.bfloat16)
        grad_query = grad_query + jnp.einsum(
            "hqk,khd->qhd", grad_scores, key_block, preferred_element_type=jnp.float32
        )
        key_part = jnp.einsum(
            "hqk,qhd->khd", grad_scores, query_heads, preferred_element_type=jnp.float32
        )
        value_part = jnp.einsum(
            "hqk,qhd->khd",
            probability.astype(jnp.bfloat16),
            grad_heads,
            preferred_element_type=jnp.float32,
        )
        keys_acc = lax.dynamic_update_slice_in_dim(
            keys_acc,
            lax.dynamic_slice_in_dim(keys_acc, first_key, KEYBLK, 0) + key_part,
            first_key,
            0,
        )
        values_acc = lax.dynamic_update_slice_in_dim(
            values_acc,
            lax.dynamic_slice_in_dim(values_acc, first_key, KEYBLK, 0) + value_part,
            first_key,
            0,
        )
        return (grad_query, keys_acc, values_acc)

    start_grad = jnp.zeros(query_heads.shape, jnp.float32)
    return lax.fori_loop(0, count_blocks, advance, (start_grad, keys_sum, values_sum))


def on_device(
    tokens,
    pair_order,
    norm_one,
    qkv_weight,
    out_weight,
    norm_two,
    gateup_weight,
    down_weight,
    cotangent,
):
    ctx_count = lax.axis_size("ctx")
    ctx_index = lax.axis_index("ctx")
    block_width = tokens.shape[1] // 2
    length = 2 * block_width * ctx_count
    scale = HEAD_DIM ** (-0.5)
    gathered = (
        lax.all_gather(norm_one, "fsdp", axis=0, tiled=True),
        lax.all_gather(qkv_weight, "fsdp", axis=0, tiled=True),
        lax.all_gather(out_weight, "fsdp", axis=0, tiled=True),
        lax.all_gather(norm_two, "fsdp", axis=0, tiled=True),
        lax.all_gather(gateup_weight, "fsdp", axis=0, tiled=True),
        lax.all_gather(down_weight, "fsdp", axis=0, tiled=True),
    )
    gain_one = gathered[0].astype(jnp.float32)
    weight_qkv = gathered[1]
    weight_out = gathered[2]
    gain_two = gathered[3].astype(jnp.float32)
    weight_gateup = gathered[4]
    weight_down = gathered[5]
    low_block = lookup(pair_order, jnp.reshape(ctx_index, (1,)))[0]
    high_block = 2 * ctx_count - 1 - low_block
    offsets = jnp.arange(block_width, dtype=jnp.int32)
    own_pos = jnp.concatenate(
        [low_block * block_width + offsets, high_block * block_width + offsets]
    )
    source = block_source(pair_order, ctx_count)
    target = block_target(pair_order, ctx_count)
    high_count = block_count(high_block, block_width)
    heads_shape = (2 * block_width, HEADS, HEAD_DIM)
    long_shape = (length, HEADS, HEAD_DIM)
    token_rows = tokens[0].astype(jnp.float32)
    normed_f, norm_pull_one = jax.vjp(layer_norm, token_rows, gain_one)
    normed = normed_f.astype(jnp.bfloat16)
    mixed_rows = jnp.dot(normed, weight_qkv, preferred_element_type=jnp.float32)
    query_rot, rope_pull = jax.vjp(partial(rotate, positions=own_pos), mixed_rows[:, :D])
    queries = query_rot.astype(jnp.bfloat16)
    keys_rot = rotate(mixed_rows[:, D : 2 * D], own_pos).astype(jnp.bfloat16)
    values = mixed_rows[:, 2 * D :].astype(jnp.bfloat16)
    all_keys = lax.all_gather(keys_rot, "ctx", axis=0, tiled=True)
    all_values = lax.all_gather(values, "ctx", axis=0, tiled=True)
    key_rows = reorder(all_keys, source, block_width).reshape(long_shape)
    value_rows = reorder(all_values, source, block_width).reshape(long_shape)
    query_heads = queries.reshape(heads_shape)
    attended_f, exact, log_total = forward_rows(
        query_heads, own_pos, key_rows, value_rows, high_count
    )
    attended = attended_f.reshape(2 * block_width, D).astype(jnp.bfloat16)
    middle = token_rows + jnp.dot(attended, weight_out, preferred_element_type=jnp.float32)
    normed_two_f, norm_pull_two = jax.vjp(layer_norm, middle, gain_two)
    normed_two = normed_two_f.astype(jnp.bfloat16)
    gateup = jnp.dot(normed_two, weight_gateup, preferred_element_type=jnp.float32)
    hidden_f, geglu_pull = jax.vjp(geglu, gateup[:, :FF], gateup[:, FF:])
    hidden = hidden_f.astype(jnp.bfloat16)
    result = middle + jnp.dot(hidden, weight_down, preferred_element_type=jnp.float32)
    outputs = [result.astype(jnp.bfloat16)]
    grad_out = cotangent[0]
    acc_down = jnp.einsum("rf,rd->fd", hidden, grad_out, preferred_element_type=jnp.float32)
    grad_hidden = jnp.einsum("rd,fd->rf", grad_out, weight_down, preferred_element_type=jnp.float32)
    grad_gate, grad_up = geglu_pull(grad_hidden)
    grad_gateup = jnp.concatenate([grad_gate, grad_up], axis=1).astype(jnp.bfloat16)
    acc_gateup = jnp.einsum(
        "rd,rf->df", normed_two, grad_gateup, preferred_element_type=jnp.float32
    )
    grad_normed_two = jnp.einsum(
        "rf,df->rd", grad_gateup, weight_gateup, preferred_element_type=jnp.float32
    )
    grad_middle_part, grad_gain_two = norm_pull_two(grad_normed_two)
    grad_middle = grad_out.astype(jnp.float32) + grad_middle_part
    grad_branch = grad_middle.astype(jnp.bfloat16)
    acc_out = jnp.einsum("rd,re->de", attended, grad_branch, preferred_element_type=jnp.float32)
    grad_attended = jnp.einsum(
        "re,de->rd", grad_branch, weight_out, preferred_element_type=jnp.float32
    ).astype(jnp.bfloat16)
    grad_heads = grad_attended.reshape(heads_shape)
    row_delta = jnp.sum(grad_heads.astype(jnp.float32) * exact, axis=-1).T
    zero_long = jnp.zeros(long_shape, jnp.float32)
    grad_query, keys_acc, values_acc = backward_rows(
        query_heads,
        own_pos,
        grad_heads,
        log_total,
        row_delta,
        key_rows,
        value_rows,
        high_count,
        zero_long,
        zero_long,
    )
    keys_home = reorder(keys_acc.reshape(length, D), target, block_width)
    values_home = reorder(values_acc.reshape(length, D), target, block_width)
    grad_keys = lax.psum_scatter(keys_home, "ctx", scatter_dimension=0, tiled=True)
    grad_values = lax.psum_scatter(values_home, "ctx", scatter_dimension=0, tiled=True)
    grad_keys = grad_keys * scale
    grad_query = grad_query.reshape(2 * block_width, D) * scale
    grad_mixed = jnp.concatenate(
        [rope_pull(grad_query)[0], rope_pull(grad_keys)[0], grad_values], axis=1
    ).astype(jnp.bfloat16)
    acc_qkv = jnp.einsum("rd,re->de", normed, grad_mixed, preferred_element_type=jnp.float32)
    grad_normed = jnp.einsum(
        "re,de->rd", grad_mixed, weight_qkv, preferred_element_type=jnp.float32
    )
    grad_rows_part, grad_gain_one = norm_pull_one(grad_normed)
    input_grads = [grad_middle + grad_rows_part]
    shares = (
        lax.psum_scatter(
            grad_gain_one.astype(jnp.bfloat16), "fsdp", scatter_dimension=0, tiled=True
        ).astype(jnp.float32),
        lax.psum_scatter(
            acc_qkv.astype(jnp.bfloat16), "fsdp", scatter_dimension=0, tiled=True
        ).astype(jnp.float32),
        lax.psum_scatter(
            acc_out.astype(jnp.bfloat16), "fsdp", scatter_dimension=0, tiled=True
        ).astype(jnp.float32),
        lax.psum_scatter(
            grad_gain_two.astype(jnp.bfloat16), "fsdp", scatter_dimension=0, tiled=True
        ).astype(jnp.float32),
        lax.psum_scatter(
            acc_gateup.astype(jnp.bfloat16), "fsdp", scatter_dimension=0, tiled=True
        ).astype(jnp.float32),
        lax.psum_scatter(
            acc_down.astype(jnp.bfloat16), "fsdp", scatter_dimension=0, tiled=True
        ).astype(jnp.float32),
    )
    totals = lax.psum((shares[0], shares[1], shares[2], shares[3], shares[4], shares[5]), "ctx")
    return (
        jnp.stack(outputs),
        jnp.stack(input_grads),
        totals[0],
        totals[1],
        totals[2],
        totals[3],
        totals[4],
        totals[5],
    )


def solution(mesh):
    return jax.shard_map(
        on_device,
        mesh=mesh,
        in_specs=(
            P("fsdp", "ctx", None),
            P(),
            P("fsdp"),
            P("fsdp", None),
            P("fsdp", None),
            P("fsdp"),
            P("fsdp", None),
            P("fsdp", None),
            P("fsdp", "ctx", None),
        ),
        out_specs=(
            P("fsdp", "ctx", None),
            P("fsdp", "ctx", None),
            P("fsdp"),
            P("fsdp", None),
            P("fsdp", None),
            P("fsdp"),
            P("fsdp", None),
            P("fsdp", None),
        ),
        check_vma=False,
    )
```

profile of v0, /device:TPU:0, one launch (start us, length us, event | category | flops | bytes accessed | tf_op | source)
XLA Modules:
  0.0 988.8 jit_solution(17419768190332207431)
XLA Ops:
  11.7 8.3 all-reduce.10
  23.0 20.0 %all-gather.7.cloned.1.call-done = bf16[768,2304]{1,0:T(8,128)(2,1)} async-done(((bf16[192,2304]{1,0:T(8,128)(2,1)}), bf16[768,2304]{1,0:T(8,128)(2,1)}) %all-gather.7.cloned.1.call-update) | async-done | bytes 3538960 | tf_op jit(solution)/shard_map/all_gather | solution.py:197
  74.0 33.8 %all-gather.9.cloned.1.call-done = bf16[2048,768]{1,0:T(8,128)(2,1)} async-done(((bf16[256,768]{1,0:T(8,128)(2,1)}), bf16[2048,768]{1,0:T(8,128)(2,1)}) %all-gather.9.cloned.1.call-update) | async-done | bytes 3145744 | tf_op jit(solution)/shard_map/all_gather | solution.py:229
  110.4 59.2 %all-gather.11.cloned.1.call-done = bf16[2048,768]{1,0:T(8,128)(2,1)} async-done(((bf16[256,768]{1,0:T(8,128)(2,1)}), bf16[2048,768]{1,0:T(8,128)(2,1)}) %all-gather.11.cloned.1.call-update) | async-done | bytes 3145744 | tf_op jit(solution)/shard_map/all_gather | solution.py:228
  189.1 15.9 %while.38 = (s32[]{:T(128)}, f32[12,256]{1,0:T(8,128)S(1)}, f32[12,256]{1,0:T(8,128)}, s32[]{:T(128)}, s32[256]{0:T(256)}, /*index=5*/bf16[2048,12,64]{0,2,1:T(8...) while((s32[]{:T(128)}, f32[12,256]{1,0:T(8,128)S(1)}, ...), condition=%wide.region_7.9_spmd, body=%wide.region_4.8_spmd.sunk | while | flops 212474368 | bytes 14419163 | solution.py:98
  210.1 5.8 reshape_reshape.12
  219.1 29.9 %while.39 = (s32[]{:T(128)}, f32[256,12,64]{0,2,1:T(8,128)}, f32[256,12,64]{0,2,1:T(8,128)}, s32[]{:T(128)}, bf16[2048,12,64]{0,2,1:T(8,128)(2,1)}, /*index=5*/s...) while((s32[]{:T(128)}, f32[256,12,64]{0,2,1:T(8,128)}, ...), condition=%wide.region_9.11_spmd, body=%wide.region_8.10_spmd.sunk | while | flops 621806080 | bytes 50419044 | solution.py:120
  284.5 55.0 %while.40 = (s32[]{:T(128)}, f32[256,12,64]{0,2,1:T(8,128)}, f32[2048,12,64]{0,2,1:T(8,128)}, f32[2048,12,64]{0,2,1:T(8,128)}, s32[]{:T(128)}, /*index=5*/bf16[2...) while((s32[]{:T(128)}, f32[256,12,64]{0,2,1:T(8,128)}, ...), condition=%wide.region_16.18_spmd, body=%wide.region_15.17_spmd.sunk | while | flops 1023476224 | bytes 48506212 | solution.py:176
  339.5 6.9 copy.115
  346.4 6.7 copy.107
  353.1 6.9 copy.114
  360.1 6.6 copy.105
  366.7 6.5 gather_fusion.3
  373.2 6.5 gather_fusion.2
  379.7 10.8 %broadcast_select_fusion.1 = (f32[16,128,768]{2,1,0:T(8,128)}, f32[16,128,768]{2,1,0:T(8,128)}) fusion(f32[16,128,768]{2,1,0:T(8,128)} %gather_fusion.2, pred[16]{0:T(512)(128)(4,1)S(1)} %copy-done.54, f32[16,128,768]{2,1,0:T(8,128)} %gather_fusion.3), kind=kLoop, calls=%fused_computation.74 | loop fusion | flops 3145728 | bytes 25165840 | tf_op jit(solution)/shard_map/jit(_take)/select_n | solution.py:67
  390.5 6.7 copy.108
  397.3 6.7 copy.106
  413.2 101.0 %reduce-scatter.9.cloned.1.call-done = f32[256,768]{0,1:T(8,128)} async-done(((f32[2048,768]{0,1:T(8,128)}), f32[256,768]{0,1:T(8,128)}) %reduce-scatter.9.cloned.1.call-update) | async-done | bytes 786448 | tf_op jit(solution)/shard_map/reduce_scatter | solution.py:281
  515.4 119.9 %reduce-scatter.7.cloned.1.call-done = f32[256,768]{0,1:T(8,128)} async-done(((f32[2048,768]{0,1:T(8,128)}), f32[256,768]{0,1:T(8,128)}) %reduce-scatter.7.cloned.1.call-update) | async-done | bytes 786448 | tf_op jit(solution)/shard_map/reduce_scatter | solution.py:280
  644.4 18.9 %reduce-scatter.13.cloned.1.call-done = bf16[192,768]{1,0:T(8,128)(2,1)} async-done(((bf16[768,768]{1,0:T(8,128)(2,1)}), bf16[192,768]{1,0:T(8,128)(2,1)}) %reduce-scatter.13.cloned.1.call-update) | async-done | bytes 294928 | tf_op jit(solution)/shard_map/reduce_scatter | solution.py:300
  663.4 32.6 %reduce-scatter.17.cloned.1.call-done = bf16[288,768]{1,0:T(8,128)(2,1)} async-done(((bf16[1152,768]{1,0:T(8,128)(2,1)}), bf16[288,768]{1,0:T(8,128)(2,1)}) %reduce-scatter.17.cloned.1.call-update) | async-done | bytes 442384 | tf_op jit(solution)/shard_map/reduce_scatter | solution.py:309
  695.9 43.1 %reduce-scatter.15.cloned.1.call-done = bf16[192,2304]{1,0:T(8,128)(2,1)} async-done(((bf16[768,2304]{1,0:T(8,128)(2,1)}), bf16[192,2304]{1,0:T(8,128)(2,1)}) %reduce-scatter.15.cloned.1.call-update) | async-done | bytes 884752 | tf_op jit(solution)/shard_map/reduce_scatter | solution.py:306
  750.0 32.1 %reduce-scatter.11.cloned.1.call-done = bf16[192,2304]{1,0:T(8,128)(2,1)} async-done(((bf16[768,2304]{1,0:T(8,128)(2,1)}), bf16[192,2304]{1,0:T(8,128)(2,1)}) %reduce-scatter.11.cloned.1.call-update) | async-done | bytes 884752 | tf_op jit(solution)/shard_map/reduce_scatter | solution.py:297
  782.1 199.6 %all-reduce.12 = (f32[192]{0:T(256)}, f32[192,2304]{1,0:T(8,128)}, f32[192,768]{1,0:T(8,128)}, f32[192]{0:T(256)}, f32[192,2304]{1,0:T(8,128)}, /*index=5*/f32[288,768]{1,0:T(8,128)}) all-reduce(f32[192]{0:T(256)S(1)} %dynamic-slice_convert_fusion.1, ...), channel_id=1, replica_groups=mesh['ctx'=8,'fsdp'=4] {'ctx'}, use_global_device_ids=true, to_apply=%region_24.27 | all-reduce | flops 1253760 | bytes 7523328 | tf_op jit(solution)/shard_map/psum | solution.py:313
  (381 shorter events, 229.8 us)
Async XLA Ops:
  7.2 35.9 %all-gather.7.cloned.1.call-start = ((), (), s32[]{:S(2)}) async-start(), calls=%async_computation.6 | async-start | bytes 4423680 | tf_op jit(solution)/shard_map/all_gather | solution.py:197
  7.9 99.9 %all-gather.9.cloned.1.call-start = ((), (), s32[]{:S(2)}) async-start(), calls=%async_computation.7 | async-start | bytes 3538944 | tf_op jit(solution)/shard_map/all_gather | solution.py:229
  20.0 26.3 %copy-start.40 = (f32[768]{0:T(1024)}, f32[768]{0:T(1024)S(1)}, u32[]{:S(2)}) copy-start(f32[768]{0:T(1024)S(1)} %convert_element_type.115) | copy-start | bytes 9220
  21.2 25.2 %copy-start.42 = (f32[256]{0:T(256)}, f32[256]{0:T(256)S(1)}, u32[]{:S(2)}) copy-start(f32[256]{0:T(256)S(1)} %broadcast_multiply_fusion.6) | copy-start | bytes 3076
  23.0 23.3 %copy-start.45 = (f32[256]{0:T(256)}, f32[256]{0:T(256)S(1)}, u32[]{:S(2)}) copy-start(f32[256]{0:T(256)S(1)} %fusion.84) | copy-start | bytes 3076
  23.0 24.2 %copy-start.55 = (s32[8]{0:T(128)S(1)}, s32[8]{0:T(128)}, u32[]{:S(2)}) copy-start(s32[8]{0:T(128)} %param.20) | copy-start | bytes 100
  47.2 122.5 %all-gather.11.cloned.1.call-start = ((), (), s32[]{:S(2)}) async-start(), calls=%async_computation.8 | async-start | bytes 3538944 | tf_op jit(solution)/shard_map/all_gather | solution.py:228
  53.8 7.4 copy-start.31
  69.4 181.6 %all-gather.13.cloned.1.call-start = ((), (), s32[]{:S(2)}) async-start(), calls=%async_computation.9 | async-start | bytes 1474560 | tf_op jit(solution)/shard_map/all_gather | solution.py:198
  70.0 184.2 %all-gather.15.cloned.1.call-start = ((), (), s32[]{:S(2)}) async-start(), calls=%async_computation.10 | async-start | bytes 4423680 | tf_op jit(solution)/shard_map/all_gather | solution.py:200
  70.6 188.4 %all-gather.17.cloned.1.call-start = ((), (), s32[]{:S(2)}) async-start(), calls=%async_computation.11 | async-start | bytes 2211840 | tf_op jit(solution)/shard_map/all_gather | solution.py:201
  71.2 443.0 %reduce-scatter.9.cloned.1.call-start = ((), (), s32[]{:S(2)}) async-start(), calls=%async_computation.13 | async-start | bytes 7077888 | tf_op jit(solution)/shard_map/reduce_scatter | solution.py:281
  397.2 238.1 %reduce-scatter.7.cloned.1.call-start = ((), (), s32[]{:S(2)}) async-start(), calls=%async_computation.12 | async-start | bytes 7077888 | tf_op jit(solution)/shard_map/reduce_scatter | solution.py:280
  404.0 259.3 %reduce-scatter.13.cloned.1.call-start = ((), (), s32[]{:S(2)}) async-start(), calls=%async_computation.15 | async-start | bytes 1474560 | tf_op jit(solution)/shard_map/reduce_scatter | solution.py:300
  406.6 289.3 %reduce-scatter.17.cloned.1.call-start = ((), (), s32[]{:S(2)}) async-start(), calls=%async_computation.17 | async-start | bytes 2211840 | tf_op jit(solution)/shard_map/reduce_scatter | solution.py:309
  408.6 330.4 %reduce-scatter.15.cloned.1.call-start = ((), (), s32[]{:S(2)}) async-start(), calls=%async_computation.16 | async-start | bytes 4423680 | tf_op jit(solution)/shard_map/reduce_scatter | solution.py:306
  411.7 370.3 %reduce-scatter.11.cloned.1.call-start = ((), (), s32[]{:S(2)}) async-start(), calls=%async_computation.14 | async-start | bytes 4423680 | tf_op jit(solution)/shard_map/reduce_scatter | solution.py:297
  413.0 223.5 %copy-start.32 = (f32[256,64]{0,1:T(8,128)S(1)}, f32[256,64]{0,1:T(8,128)}, u32[]{:S(2)}) copy-start(f32[256,64]{0,1:T(8,128)} %copy-done.31) | copy-start | bytes 196612
  515.4 121.4 %copy-start.34 = (f32[256,64]{0,1:T(8,128)S(1)}, f32[256,64]{0,1:T(8,128)}, u32[]{:S(2)}) copy-start(f32[256,64]{0,1:T(8,128)} %copy-done.33) | copy-start | bytes 196612
  644.4 97.9 %copy-start.50 = (f32[256]{0:T(256)S(1)}, f32[256]{0:T(256)}, u32[]{:S(2)}) copy-start(f32[256]{0:T(256)} %copy-done.49) | copy-start | bytes 3076
  644.4 98.4 %copy-start.53 = (bf16[768]{0:T(1024)(128)(2,1)S(1)}, bf16[768]{0:T(1024)(128)(2,1)}, u32[]{:S(2)}) copy-start(bf16[768]{0:T(1024)(128)(2,1)} %get-tuple-element.198) | copy-start | bytes 4612
  644.4 104.3 %copy-start.9 = (f32[256,768]{1,0:T(8,128)S(1)}, f32[256,768]{1,0:T(8,128)}, u32[]{:S(2)}) copy-start(f32[256,768]{1,0:T(8,128)} %copy-done.8) | copy-start | bytes 2359300
  644.4 104.3 %copy-start.52 = (f32[256]{0:T(256)S(1)}, f32[256]{0:T(256)}, u32[]{:S(2)}) copy-start(f32[256]{0:T(256)} %copy-done.51) | copy-start | bytes 3076
  742.3 39.7 %copy-start.26 = (bf16[192,2304]{1,0:T(8,128)(2,1)S(1)}, bf16[192,2304]{1,0:T(8,128)(2,1)}, u32[]{:S(2)}) copy-start(bf16[192,2304]{1,0:T(8,128)(2,1)} %reduce-scatter.15.cloned.1.call-done) | copy-start | bytes 2654212
  (83 other events, 163.7 us)
Sparse Core Ops, SparseCore 0:
  9.6 33.4 all-gather.6
  47.3 60.4 all-gather.8
  110.6 59.0 all-gather.10
  171.1 16.0 all-gather.12
  188.6 30.7 all-gather.14
  220.8 20.8 all-gather.16
  397.4 116.7 reduce-scatter.8
  517.8 117.4 reduce-scatter.6
  638.5 24.8 reduce-scatter.12
  666.5 29.3 reduce-scatter.16
  698.5 40.4 reduce-scatter.14
  741.6 40.4 reduce-scatter.10
where the time goes:
time: 998 us; the launch traced here: 989 us
  waiting for transfers between devices  463 us (46%)
  blocking collectives  214 us (21%)
  local copies, waits for them, and re-layouts  128 us (13%)
  matrix products  111 us (11%)
  other arithmetic  52.7 us (5%)
  between operations  18.4 us (2%)
    psum x1, blocking collectives, on_device(): lax.psum((shares[0], shares[1], shares[2], shares[3], shares[4], shares[5...  200 us
    reduce_scatter x1, waiting for transfers between devices, on_device(): lax.psum_scatter(keys_home, 'ctx', scatter_dimension=0, tiled=True)  120 us
    reduce_scatter x1, waiting for transfers between devices, on_device(): lax.psum_scatter(values_home, 'ctx', scatter_dimension=0, tiled=True)  101 us
    all_gather x1, waiting for transfers between devices, on_device(): all_keys = lax.all_gather(keys_rot, 'ctx', axis=0, tiled=True)  59.2 us
    reduce_scatter x1, waiting for transfers between devices, on_device(): lax.psum_scatter(acc_gateup.astype(jnp.bfloat16), 'fsdp', scatter_dimensi...  43.1 us
    all_gather x1, waiting for transfers between devices, on_device(): all_values = lax.all_gather(values, 'ctx', axis=0, tiled=True)  33.8 us
    reduce_scatter x1, waiting for transfers between devices, on_device(): lax.psum_scatter(acc_down.astype(jnp.bfloat16), 'fsdp', scatter_dimension...  32.6 us
    reduce_scatter x1, waiting for transfers between devices, on_device(): lax.psum_scatter(acc_qkv.astype(jnp.bfloat16), 'fsdp', scatter_dimension=...  32.1 us
  transfers between devices with their start and end apart: 12, of which 9 were waited for; matrix products, arithmetic and copies ran while one was open for 14% of the time, Pallas kernels for 0%

commit v1 on v0

v1 whole, which is shorter than its diff:
```python
from functools import partial

import jax
import jax.numpy as jnp
from jax import lax
from jax.experimental import pallas as pl
from jax.experimental.pallas import tpu as pltpu
from jax.sharding import PartitionSpec as P

D = 768
HEAD_DIM = 64
FF = 1152
LANES = 128
PAIRS = D // LANES
COLS = 256
SCALE = HEAD_DIM**-0.5

theta_base = 160000.0
norm_eps = 1e-05
neg_large = -1e30
f32 = jnp.float32
bf16 = jnp.bfloat16

SMEM = pl.BlockSpec(memory_space=pltpu.SMEM)
WHOLE = pl.BlockSpec(memory_space=pltpu.VMEM)


def params(megabytes):
    return pltpu.CompilerParams(vmem_limit_bytes=megabytes * 2**20)


def cost(flops, moved, exps=0):
    return pl.CostEstimate(flops=int(flops), bytes_accessed=int(moved), transcendentals=int(exps))


def dot(left, right, left_dim, right_dim):
    return lax.dot_general(
        left, right, (((left_dim,), (right_dim,)), ((), ())), preferred_element_type=f32
    )


def ring_device(place, count):
    return jnp.where(place < count // 2, 2 * place, 2 * (count - 1 - place) + 1)


def ring_place(device, count):
    return jnp.where(device % 2 == 0, device // 2, count - 1 - device // 2)


def shift(array, step, count):
    half = count // 2
    order = [2 * i if i < half else 2 * (count - 1 - i) + 1 for i in range(count)]
    pairs = [(order[i], order[(i + step) % count]) for i in range(count)]
    return lax.ppermute(array, "ctx", pairs)


def ring_offsets(count):
    half = count // 2
    offsets = [0]
    for distance in range(1, half):
        offsets += [-distance, distance]
    return offsets + [half]


def ring_gather(first, second, count):
    half = count // 2
    firsts, seconds = [first], [second]
    up, down = (first, second), (first, second)
    for _ in range(1, half):
        up = tuple(shift(part, 1, count) for part in up)
        down = tuple(shift(part, -1, count) for part in down)
        firsts += [up[0], down[0]]
        seconds += [up[1], down[1]]
    firsts.append(shift(up[0], 1, count))
    seconds.append(shift(down[1], -1, count))
    return firsts, seconds


def add_rounded(left, right):
    return (left.astype(f32) + right.astype(f32)).astype(bf16)


def ring_scatter(firsts, seconds, count):
    half = count // 2
    places = {offset: slot for slot, offset in enumerate(ring_offsets(count))}
    down = [shift(firsts[-1], -1, count), None]
    up = [None, shift(seconds[-1], 1, count)]
    for distance in range(half - 1, 0, -1):
        for side, sums in ((-1, down), (1, up)):
            slot = places[side * distance]
            for which, parts in enumerate((firsts, seconds)):
                part = parts[slot]
                if sums[which] is not None:
                    part = add_rounded(part, sums[which])
                sums[which] = shift(part, side, count)
    return (firsts[0], down[0], up[0]), (seconds[0], down[1], up[1])


def ring_total(rows, count):
    height, width = rows.shape
    if height % (8 * count) or width % LANES:
        return lax.psum(rows, "ctx").astype(f32)
    part = height // count
    cut = (width // LANES + 1) // 2 * LANES
    place = ring_place(lax.axis_index("ctx"), count)
    pieces = []
    for offset in ring_offsets(count):
        start = ((place + offset) % count) * part
        pieces.append(lax.dynamic_slice_in_dim(rows, start, part, 0))
    firsts = [piece[:, :cut] for piece in pieces]
    seconds = [piece[:, cut:] for piece in pieces]
    sums = ring_scatter(firsts, seconds, count)
    first, second = (
        (own.astype(f32) + one.astype(f32) + other.astype(f32)).astype(bf16)
        for own, one, other in sums
    )
    firsts, seconds = ring_gather(first, second, count)
    by_offset = {offset % count: slot for slot, offset in enumerate(ring_offsets(count))}
    line = [
        jnp.concatenate([firsts[by_offset[i]], seconds[by_offset[i]]], axis=1)
        for i in range(count)
    ]
    twice = jnp.concatenate(line + line, axis=0)
    return lax.dynamic_slice_in_dim(
        twice, ((count - place) % count) * part, height, 0
    ).astype(f32)


def swap(array, mask):
    return lax.ppermute(array, "fsdp", [(i, i ^ mask) for i in range(4)])


def gather_pieces(piece):
    far = swap(piece, 2)
    return [piece, swap(piece, 1), far, swap(far, 1)]


def scatter_pieces(pieces):
    far = add_rounded(pieces[2], swap(pieces[3], 1))
    near = swap(pieces[1], 1)
    return (pieces[0].astype(f32) + near.astype(f32) + swap(far, 2).astype(f32)).astype(bf16)


def in_order(pieces, me):
    odd = (me % 2) == 1
    high = (me // 2) == 1
    low_pair = [jnp.where(odd, pieces[1], pieces[0]), jnp.where(odd, pieces[0], pieces[1])]
    high_pair = [jnp.where(odd, pieces[3], pieces[2]), jnp.where(odd, pieces[2], pieces[3])]
    first = [jnp.where(high, b, a) for a, b in zip(low_pair, high_pair)]
    last = [jnp.where(high, a, b) for a, b in zip(low_pair, high_pair)]
    return jnp.concatenate(first + last, axis=0)


def out_of_order(whole, me):
    rows = whole.shape[0] // 4
    return [lax.dynamic_slice_in_dim(whole, (me ^ i) * rows, rows, 0) for i in range(4)]


def swap_halves(block):
    lane = lax.broadcasted_iota(jnp.int32, block.shape, 1)
    ahead = pltpu.roll(block, block.shape[1] - HEAD_DIM // 2, 1)
    behind = pltpu.roll(block, HEAD_DIM // 2, 1)
    return jnp.where(lane % HEAD_DIM < HEAD_DIM // 2, ahead, behind)


def normalise(rows):
    mean_value = jnp.mean(rows, axis=-1, keepdims=True)
    centered = rows - mean_value
    spread = jnp.mean(centered * centered, axis=-1, keepdims=True)
    inverse = lax.rsqrt(spread + norm_eps)
    return centered * inverse, inverse


def kv_kernel(me, tokens, gains, w0, w1, w2, w3, cosine, sine, keys, values, normed, gain_by):
    step = pl.program_id(0)
    quarter = D // 4
    mine = me[0]

    @pl.when(step == 0)
    def _():
        unit, _ = normalise(tokens[...].astype(f32))
        for i in range(4):
            gain_by[mine ^ i] = gains[i, 0:1, :]
        for i in range(4):
            normed[i] = (unit[:, i * quarter : (i + 1) * quarter] * gain_by[i]).astype(bf16)

    total = None
    for i, weight in enumerate((w0, w1, w2, w3)):
        part = dot(normed[mine ^ i], weight[...], 1, 0)
        total = part if total is None else total + part
    half = pl.num_programs(0) // 2

    @pl.when(step < half)
    def _():
        for i in range(COLS // LANES):
            columns = slice(i * LANES, (i + 1) * LANES)
            block = total[:, columns]
            keys[:, columns] = (
                block * cosine[...] + swap_halves(block) * sine[...]
            ).astype(bf16)

    @pl.when(step >= half)
    def _():
        values[...] = total.astype(bf16)


def project_kv(me, tokens, gains, weights, cosine, sine):
    rows = tokens.shape[0]
    half = D // COLS

    def fixed(*shape):
        return pl.BlockSpec(shape, lambda j: (0,) * len(shape))

    return pl.pallas_call(
        kv_kernel,
        grid=(2 * half,),
        in_specs=[SMEM, fixed(rows, D), fixed(*gains.shape)]
        + [pl.BlockSpec((D // 4, COLS), lambda j: (0, j))] * 4
        + [fixed(rows, LANES)] * 2,
        out_specs=[
            pl.BlockSpec((rows, COLS), lambda j: (0, jnp.minimum(j, half - 1))),
            pl.BlockSpec((rows, COLS), lambda j: (0, jnp.maximum(j - half, 0))),
            fixed(4, rows, D // 4),
        ],
        out_shape=[
            jax.ShapeDtypeStruct((rows, D), bf16),
            jax.ShapeDtypeStruct((rows, D), bf16),
            jax.ShapeDtypeStruct((4, rows, D // 4), bf16),
        ],
        scratch_shapes=[pltpu.VMEM((4, 1, D // 4), f32)],
        compiler_params=params(32),
        cost_estimate=cost(4 * rows * D * D, 4 * D * D),
        name="project_kv",
    )(me, tokens, gains, *weights, cosine, sine)


def q_kernel(me, normed, w0, w1, w2, w3, cosine, sine, queries):
    mine = me[0]
    total = None
    for i, weight in enumerate((w0, w1, w2, w3)):
        part = dot(normed[mine ^ i], weight[...], 1, 0)
        total = part if total is None else total + part
    for i in range(COLS // LANES):
        columns = slice(i * LANES, (i + 1) * LANES)
        block = total[:, columns]
        queries[:, columns] = (block * cosine[...] + swap_halves(block) * sine[...]).astype(bf16)


def project_q(me, normed, weights, cosine, sine):
    rows = normed.shape[1]

    def fixed(*shape):
        return pl.BlockSpec(shape, lambda j: (0,) * len(shape))

    return pl.pallas_call(
        q_kernel,
        grid=(D // COLS,),
        in_specs=[SMEM, fixed(4, rows, D // 4)]
        + [pl.BlockSpec((D // 4, COLS), lambda j: (0, j))] * 4
        + [fixed(rows, LANES)] * 2,
        out_specs=pl.BlockSpec((rows, COLS), lambda j: (0, j)),
        out_shape=jax.ShapeDtypeStruct((rows, D), bf16),
        compiler_params=params(32),
        cost_estimate=cost(2 * rows * D * D, 2 * D * D),
        name="project_q",
    )(me, normed, *weights, cosine, sine)


def stacked(block, factor=None):
    if factor is not None:
        block = block * jnp.asarray(factor, block.dtype)
    lane = lax.broadcasted_iota(jnp.int32, block.shape, 1)
    zero = jnp.zeros_like(block)
    return jnp.concatenate(
        [jnp.where(lane < HEAD_DIM, block, zero), jnp.where(lane < HEAD_DIM, zero, block)], axis=0
    )


def unstacked(block):
    rows = block.shape[0] // 2
    lane = lax.broadcasted_iota(jnp.int32, (rows, block.shape[1]), 1)
    return jnp.where(lane < HEAD_DIM, block[:rows], block[rows:])


def causal(scores):
    rows, columns = scores.shape
    row = lax.broadcasted_iota(jnp.int32, scores.shape, 0) % (rows // 2)
    column = lax.broadcasted_iota(jnp.int32, scores.shape, 1)
    return jnp.where(column <= row, scores, neg_large)


def over_chunks(groups, per, visit):
    for group in range(groups):
        first = 1 if group == 0 else 0
        if per == 1:
            if first == 0:
                visit(group, 0, group)
        else:

            def turn(i, carry, group=group):
                visit(group, i, group * per + i)
                return carry

            lax.fori_loop(first, per, turn, 0)


def attend_kernel(groups, per, blocks, queries, *refs):
    keys, values = refs[:groups], refs[groups : 2 * groups]
    attended, exact, log_total, stack, scores, tops, totals, coarse_sum, fine_sum = refs[2 * groups :]
    width = queries.shape[0] // 2
    own = blocks[0]
    low, high = slice(0, width), slice(width, 2 * width)

    def picked(chunk):
        which = (blocks[chunk] > own).astype(jnp.int32)
        return which, pl.ds(pl.multiple_of(which * width, width), width)

    for i in range(2):
        stack[i] = stacked(queries[i * width : (i + 1) * width, :], SCALE)

    first = causal(dot(stack[0], keys[0][0, low, :], 1, 1))
    second = causal(dot(stack[1], keys[0][0, high, :], 1, 1))
    third = dot(stack[1], keys[0][0, low, :], 1, 1)
    scores[0], scores[1], scores[2] = first, second, third
    tops[0] = first
    tops[1] = jnp.maximum(second, third)

    def score(group, i, chunk):
        which, rows = picked(chunk)
        full = dot(stack[1], keys[group][i, low, :], 1, 1)
        scores[2 * chunk + 1] = full
        tops[1] = jnp.maximum(tops[1], full)
        part = dot(stack[which], keys[group][i, rows, :], 1, 1)
        scores[2 * chunk + 2] = part
        tops[which] = jnp.maximum(tops[which], part)

    over_chunks(groups, per, score)
    for i in range(2):
        tops[i] = jnp.broadcast_to(jnp.max(tops[i], axis=1, keepdims=True), tops.shape[1:])

    for i in range(3):
        scores[i] = jnp.exp(scores[i] - tops[min(i, 1)])
    totals[0] = scores[0]
    totals[1] = scores[1] + scores[2]

    def exponent(group, i, chunk):
        which, _ = picked(chunk)
        full = jnp.exp(scores[2 * chunk + 1] - tops[1])
        scores[2 * chunk + 1] = full
        totals[1] += full
        part = jnp.exp(scores[2 * chunk + 2] - tops[which])
        scores[2 * chunk + 2] = part
        totals[which] += part

    over_chunks(groups, per, exponent)
    for i in range(2):
        total = jnp.broadcast_to(jnp.sum(totals[i], axis=1, keepdims=True), totals.shape[1:])
        log_total[0, i] = tops[i] + jnp.log(total)
        totals[i] = 1.0 / total

    def weigh(slot, which, value_rows):
        probability = scores[slot] * totals[which]
        coarse = probability.astype(bf16)
        remainder = (probability - coarse.astype(f32)).astype(bf16)
        return dot(coarse, value_rows, 1, 0), dot(remainder, value_rows, 1, 0)

    coarse_sum[0], fine_sum[0] = weigh(0, 0, values[0][0, low, :])
    one = weigh(1, 1, values[0][0, high, :])
    two = weigh(2, 1, values[0][0, low, :])
    coarse_sum[1], fine_sum[1] = one[0] + two[0], one[1] + two[1]

    def collect(group, i, chunk):
        which, rows = picked(chunk)
        coarse, fine = weigh(2 * chunk + 1, 1, values[group][i, low, :])
        coarse_sum[1] += coarse
        fine_sum[1] += fine
        coarse, fine = weigh(2 * chunk + 2, which, values[group][i, rows, :])
        coarse_sum[which] += coarse
        fine_sum[which] += fine

    over_chunks(groups, per, collect)
    for i, rows in enumerate((low, high)):
        attended[rows, :] = unstacked(coarse_sum[i]).astype(bf16)
        exact[rows, :] = unstacked(coarse_sum[i] + fine_sum[i])


def attend(blocks, queries, keys, values):
    rows = queries.shape[0]
    groups, per = len(keys), keys[0].shape[0]
    count = groups * per
    column = pl.BlockSpec((rows, LANES), lambda j: (0, j))
    chunk = pl.BlockSpec((per, rows, LANES), lambda j: (0, 0, j))
    stat = pltpu.VMEM((2, rows, LANES), f32)
    return pl.pallas_call(
        partial(attend_kernel, groups, per),
        grid=(PAIRS,),
        in_specs=[SMEM, column] + [chunk] * (2 * groups),
        out_specs=[column, column, pl.BlockSpec((1, 2, rows, LANES), lambda j: (j, 0, 0, 0))],
        out_shape=[
            jax.ShapeDtypeStruct((rows, D), bf16),
            jax.ShapeDtypeStruct((rows, D), f32),
            jax.ShapeDtypeStruct((PAIRS, 2, rows, LANES), f32),
        ],
        scratch_shapes=[
            pltpu.VMEM((2, rows, LANES), bf16),
            pltpu.VMEM((2 * count + 1, rows, LANES), f32),
            stat,
            stat,
            stat,
            stat,
        ],
        compiler_params=params(56),
        cost_estimate=cost(6 * rows * rows * count * D, 4 * rows * count * D, rows * rows * 6 * count),
        name="attend",
    )(blocks, queries, *keys, *values)


def attend_back_kernel(groups, per, blocks, queries, grads, exact, log_total, cosine, sine, *refs):
    keys, values = refs[:groups], refs[groups : 2 * groups]
    grad_queries = refs[2 * groups]
    grad_keys = refs[2 * groups + 1 : 3 * groups + 1]
    grad_values = refs[3 * groups + 1 : 4 * groups + 1]
    stack, grad_stack, deltas, query_sum = refs[4 * groups + 1 :]
    width = queries.shape[0] // 2
    own = blocks[0]
    low, high = slice(0, width), slice(width, 2 * width)

    for i, rows in enumerate((low, high)):
        stack[i] = stacked(queries[rows, :], SCALE)
        grad_rows = stacked(grads[rows, :])
        grad_stack[i] = grad_rows
        twice = jnp.concatenate([exact[rows, :], exact[rows, :]], axis=0)
        delta = jnp.sum(grad_rows.astype(f32) * twice, axis=1, keepdims=True)
        deltas[i] = jnp.broadcast_to(delta, deltas.shape[1:])

    def block(which, key_rows, value_rows, diagonal=False):
        query_rows, grad_rows = stack[which], grad_stack[which]
        raw = dot(query_rows, key_rows, 1, 1)
        if diagonal:
            raw = causal(raw)
        probability = jnp.exp(raw - log_total[0, which])
        grad_prob = dot(grad_rows, value_rows, 1, 1)
        grad_scores = (probability * (grad_prob - deltas[which])).astype(bf16)
        return (
            dot(grad_scores, key_rows, 1, 0),
            dot(grad_scores, query_rows, 0, 0),
            dot(probability.astype(bf16), grad_rows, 0, 0),
        )

    key_low, value_low = keys[0][0, low, :], values[0][0, low, :]
    query_one, key_one, value_one = block(0, key_low, value_low, True)
    query_two, key_two, value_two = block(1, keys[0][0, high, :], values[0][0, high, :], True)
    query_all, key_all, value_all = block(1, key_low, value_low)
    query_sum[0] = query_one
    query_sum[1] = query_two + query_all
    grad_keys[0][0, low, :] = (key_one + key_all).astype(bf16)
    grad_values[0][0, low, :] = (value_one + value_all).astype(bf16)
    grad_keys[0][0, high, :] = key_two.astype(bf16)
    grad_values[0][0, high, :] = value_two.astype(bf16)

    def visit(group, i, chunk):
        up = blocks[chunk] > own
        which = up.astype(jnp.int32)
        rows = pl.ds(pl.multiple_of(which * width, width), width)
        query_all, key_all, value_all = block(1, keys[group][i, low, :], values[group][i, low, :])
        query_sum[1] += query_all
        query_one, key_one, value_one = block(
            which, keys[group][i, rows, :], values[group][i, rows, :]
        )
        query_sum[which] += query_one
        for target, whole, part in (
            (grad_keys[group], key_all, key_one),
            (grad_values[group], value_all, value_one),
        ):
            zero = jnp.zeros_like(part)
            target[i, low, :] = (whole + jnp.where(up, zero, part)).astype(bf16)
            target[i, high, :] = jnp.where(up, part, zero).astype(bf16)

    over_chunks(groups, per, visit)
    for i, rows in enumerate((low, high)):
        grad = unstacked(query_sum[i]) * SCALE
        turned = grad * cosine[rows, :] - swap_halves(grad) * sine[rows, :]
        grad_queries[rows, :] = turned.astype(bf16)


def attend_back(blocks, queries, grads, exact, log_total, cosine, sine, keys, values):
    rows = queries.shape[0]
    groups, per = len(keys), keys[0].shape[0]
    count = groups * per
    column = pl.BlockSpec((rows, LANES), lambda j: (0, j))
    table = pl.BlockSpec((rows, LANES), lambda j: (0, 0))
    chunk = pl.BlockSpec((per, rows, LANES), lambda j: (0, 0, j))
    stat = pltpu.VMEM((2, rows, LANES), f32)
    half = pltpu.VMEM((2, rows, LANES), bf16)
    result = pl.pallas_call(
        partial(attend_back_kernel, groups, per),
        grid=(PAIRS,),
        in_specs=[SMEM, column, column, column]
        + [pl.BlockSpec((1, 2, rows, LANES), lambda j: (j, 0, 0, 0)), table, table]
        + [chunk] * (2 * groups),
        out_specs=[column] + [chunk] * (2 * groups),
        out_shape=[jax.ShapeDtypeStruct((rows, D), bf16)]
        + [jax.ShapeDtypeStruct((per, rows, D), bf16)] * (2 * groups),
        scratch_shapes=[half, half, stat, stat],
        compiler_params=params(56),
        cost_estimate=cost(10 * rows * rows * count * D, 8 * rows * count * D, rows * rows * 6 * count),
        name="attend_back",
    )(blocks, queries, grads, exact, log_total, cosine, sine, *keys, *values)
    return result[0], result[1 : groups + 1], result[groups + 1 :]


def q_back_kernel(me, normed, grads, w0, w1, w2, w3, g0, g1, g2, g3, back):
    mine = me[0]
    step = pl.program_id(0)
    block = grads[...]
    for i, (weight, target) in enumerate(((w0, g0), (w1, g1), (w2, g2), (w3, g3))):
        target[...] = dot(normed[mine ^ i], block, 0, 0).astype(bf16)
        part = dot(block, weight[...], 1, 1)

        @pl.when(step == 0)
        def _(i=i, part=part):
            back[mine ^ i] = part

        @pl.when(step > 0)
        def _(i=i, part=part):
            back[mine ^ i] += part


def q_back(me, normed, grads, weights):
    rows = grads.shape[0]

    def fixed(*shape):
        return pl.BlockSpec(shape, lambda j: (0,) * len(shape))

    column = pl.BlockSpec((D // 4, COLS), lambda j: (0, j))
    result = pl.pallas_call(
        q_back_kernel,
        grid=(D // COLS,),
        in_specs=[SMEM, fixed(4, rows, D // 4), pl.BlockSpec((rows, COLS), lambda j: (0, j))]
        + [column] * 4,
        out_specs=[column] * 4 + [fixed(4, rows, D // 4)],
        out_shape=[jax.ShapeDtypeStruct((D // 4, D), bf16)] * 4
        + [jax.ShapeDtypeStruct((4, rows, D // 4), f32)],
        compiler_params=params(32),
        cost_estimate=cost(4 * rows * D * D, 4 * D * D),
        name="q_back",
    )(me, normed, grads, *weights)
    return result[:4], result[4]


def kv_back_kernel(
    me, normed, k_own, k_one, k_two, v_own, v_one, v_two, w0, w1, w2, w3, cosine, sine,
    start, tokens, gains, grad_middle, g0, g1, g2, g3, grad_tokens, grad_gain, back, gain_by, block_of,
):
    mine = me[0]
    step = pl.program_id(0)
    last = pl.num_programs(0) - 1
    half = pl.num_programs(0) // 2
    quarter = D // 4

    @pl.when(step == 0)
    def _():
        back[...] = start[...]

    @pl.when(step < half)
    def _():
        total = k_own[...].astype(f32) + k_one[...].astype(f32) + k_two[...].astype(f32)
        for i in range(COLS // LANES):
            columns = slice(i * LANES, (i + 1) * LANES)
            part = total[:, columns]
            turned = part * cosine[...] - swap_halves(part) * sine[...]
            block_of[:, columns] = turned.astype(bf16)

    @pl.when(step >= half)
    def _():
        total = v_own[...].astype(f32) + v_one[...].astype(f32) + v_two[...].astype(f32)
        block_of[...] = total.astype(bf16)

    block = block_of[...]
    for i, (weight, target) in enumerate(((w0, g0), (w1, g1), (w2, g2), (w3, g3))):
        target[...] = dot(normed[mine ^ i], block, 0, 0).astype(bf16)
        back[mine ^ i] += dot(block, weight[...], 1, 1)

    @pl.when(step == last)
    def _():
        unit, inverse = normalise(tokens[...].astype(f32))
        for i in range(4):
            gain_by[mine ^ i] = gains[i, 0:1, :]
        incoming = jnp.concatenate([back[i] for i in range(4)], axis=1)
        gain = jnp.concatenate([gain_by[i] for i in range(4)], axis=1)
        grad_gain[...] = jnp.sum(incoming * unit, axis=0, keepdims=True)
        scaled = incoming * gain
        mean_one = jnp.mean(scaled, axis=-1, keepdims=True)
        mean_two = jnp.mean(scaled * unit, axis=-1, keepdims=True)
        grad_tokens[...] = grad_middle[...] + inverse * (scaled - mean_one - unit * mean_two)


def kv_back(me, normed, key_sums, value_sums, weights, cosine, sine, start, tokens, gains, grad_middle):
    rows = tokens.shape[0]
    half = D // COLS

    def fixed(*shape):
        return pl.BlockSpec(shape, lambda j: (0,) * len(shape))

    column = pl.BlockSpec((D // 4, COLS), lambda j: (0, j))
    key_block = pl.BlockSpec((rows, COLS), lambda j: (0, jnp.minimum(j, half - 1)))
    value_block = pl.BlockSpec((rows, COLS), lambda j: (0, jnp.maximum(j - half, 0)))
    result = pl.pallas_call(
        kv_back_kernel,
        grid=(2 * half,),
        in_specs=[SMEM, fixed(4, rows, D // 4)]
        + [key_block] * 3
        + [value_block] * 3
        + [column] * 4
        + [fixed(rows, LANES)] * 2
        + [fixed(4, rows, D // 4), fixed(rows, D), fixed(*gains.shape), fixed(rows, D)],
        out_specs=[column] * 4 + [fixed(rows, D), fixed(1, D)],
        out_shape=[jax.ShapeDtypeStruct((D // 4, 2 * D), bf16)] * 4
        + [jax.ShapeDtypeStruct((rows, D), f32), jax.ShapeDtypeStruct((1, D), f32)],
        scratch_shapes=[
            pltpu.VMEM((4, rows, D // 4), f32),
            pltpu.VMEM((4, 1, D // 4), f32),
            pltpu.VMEM((rows, COLS), bf16),
        ],
        compiler_params=params(32),
        cost_estimate=cost(8 * rows * D * D, 8 * D * D),
        name="kv_back",
    )(me, normed, *key_sums, *value_sums, *weights, cosine, sine, start, tokens, gains, grad_middle)
    return result[:4], result[4], result[5]


def layer_norm(token_rows, gain_row):
    mean_value = jnp.mean(token_rows, axis=-1, keepdims=True)
    centered = token_rows - mean_value
    spread = jnp.mean(centered * centered, axis=-1, keepdims=True)
    return centered * lax.rsqrt(spread + norm_eps) * gain_row


def geglu(gate_part, up_part):
    return jax.nn.gelu(gate_part, approximate=False) * up_part


def rope_tables(positions):
    half = HEAD_DIM // 2
    frequency = theta_base ** (-2.0 * jnp.arange(half, dtype=f32) / HEAD_DIM)
    angles = positions.astype(f32)[:, None] * frequency[None, :]
    cosine, sine = jnp.cos(angles), jnp.sin(angles)
    return (
        jnp.concatenate([cosine] * 4, axis=1),
        jnp.concatenate([-sine, sine, -sine, sine], axis=1),
    )


def on_device(
    tokens,
    pair_order,
    norm_one,
    qkv_weight,
    out_weight,
    norm_two,
    gateup_weight,
    down_weight,
    cotangent,
):
    count = lax.axis_size("ctx")
    me = lax.axis_index("fsdp")
    me_row = jnp.reshape(me, (1,)).astype(jnp.int32)
    place = ring_place(lax.axis_index("ctx"), count)
    width = tokens.shape[1] // 2
    offsets = jnp.asarray(ring_offsets(count), jnp.int32)
    chunk_devices = ring_device((place + offsets) % count, count)
    blocks = jnp.sum(
        jnp.where(
            chunk_devices[:, None] == jnp.arange(count, dtype=jnp.int32)[None, :],
            pair_order[None, :],
            0,
        ),
        axis=1,
    )
    low_block = blocks[0]
    high_block = 2 * count - 1 - low_block
    within = jnp.arange(width, dtype=jnp.int32)
    positions = jnp.concatenate([low_block * width + within, high_block * width + within])
    cosine, sine = rope_tables(positions)

    gains = jnp.stack(gather_pieces(jnp.stack([norm_one, norm_two]).astype(f32)))
    kv_weights = gather_pieces(qkv_weight[:, D:])
    q_weights = gather_pieces(qkv_weight[:, :D])
    out_pieces = gather_pieces(out_weight)
    gateup_pieces = gather_pieces(gateup_weight)
    down_pieces = gather_pieces(down_weight)

    token_rows = tokens[0]
    keys, values, normed = project_kv(me_row, token_rows, gains, kv_weights, cosine, sine)
    all_keys, all_values = ring_gather(keys, values, count)
    queries = project_q(me_row, normed, q_weights, cosine, sine)
    per = max(1, count // 8)
    group_keys = [jnp.stack(all_keys[i : i + per]) for i in range(0, count, per)]
    group_values = [jnp.stack(all_values[i : i + per]) for i in range(0, count, per)]
    attended, exact, log_total = attend(blocks, queries, group_keys, group_values)

    weight_out = in_order(out_pieces, me)
    weight_gateup = in_order(gateup_pieces, me)
    weight_down = in_order(down_pieces, me)
    gain_two = in_order([gains[i, 1] for i in range(4)], me)
    middle = token_rows.astype(f32) + jnp.dot(attended, weight_out, preferred_element_type=f32)
    normed_two_f, norm_pull_two = jax.vjp(layer_norm, middle, gain_two)
    normed_two = normed_two_f.astype(bf16)
    gateup = jnp.dot(normed_two, weight_gateup, preferred_element_type=f32)
    hidden_f, geglu_pull = jax.vjp(geglu, gateup[:, :FF], gateup[:, FF:])
    hidden = hidden_f.astype(bf16)
    result = middle + jnp.dot(hidden, weight_down, preferred_element_type=f32)
    grad_out = cotangent[0]
    acc_down = dot(hidden, grad_out, 0, 0).astype(bf16)
    grad_hidden = dot(grad_out, weight_down, 1, 1)
    grad_gate, grad_up = geglu_pull(grad_hidden)
    grad_gateup = jnp.concatenate([grad_gate, grad_up], axis=1).astype(bf16)
    acc_gateup = dot(normed_two, grad_gateup, 0, 0).astype(bf16)
    grad_normed_two = dot(grad_gateup, weight_gateup, 1, 1)
    grad_middle_part, grad_gain_two = norm_pull_two(grad_normed_two)
    grad_middle = grad_out.astype(f32) + grad_middle_part
    grad_branch = grad_middle.astype(bf16)
    acc_out = dot(attended, grad_branch, 0, 0).astype(bf16)
    grad_attended = dot(grad_branch, weight_out, 1, 1).astype(bf16)

    grad_queries, key_grads, value_grads = attend_back(
        blocks, queries, grad_attended, exact, log_total, cosine, sine, group_keys, group_values
    )
    key_list = [part[i] for part in key_grads for i in range(per)]
    value_list = [part[i] for part in value_grads for i in range(per)]
    key_sums, value_sums = ring_scatter(key_list, value_list, count)
    q_pieces, start = q_back(me_row, normed, grad_queries, q_weights)

    def fold(piece):
        top, rest = piece[: D // 4], piece[D // 4 :]
        return jnp.concatenate(
            [top, jnp.concatenate([rest[:, : D // 2], rest[:, D // 2 :]], axis=0)], axis=1
        )

    def unfold(piece):
        top, rest = piece[:, :D], piece[:, D:]
        return jnp.concatenate(
            [top, jnp.concatenate([rest[: D // 8], rest[D // 8 :]], axis=1)], axis=0
        )

    packed = [
        jnp.concatenate([part[0], part[1], fold(part[2]), part[3]], axis=1)
        for part in zip(
            out_of_order(acc_gateup, me), out_of_order(acc_out, me), out_of_order(acc_down, me), q_pieces
        )
    ]
    middle_total = ring_total(scatter_pieces(packed), count)

    kv_pieces, grad_tokens, grad_gain_one = kv_back(
        me_row, normed, key_sums, value_sums, kv_weights, cosine, sine, start, token_rows, gains, grad_middle
    )
    kv_total = ring_total(scatter_pieces(kv_pieces), count)
    gain_grads = lax.psum(jnp.stack([grad_gain_one[0], grad_gain_two]), ("ctx", "fsdp"))
    gain_own = lax.dynamic_slice_in_dim(gain_grads, me * (D // 4), D // 4, 1)
    ends = (3 * D, 4 * D, 4 * D + FF, 5 * D + FF)
    return (
        result.astype(bf16)[None],
        grad_tokens[None],
        gain_own[0],
        jnp.concatenate([middle_total[:, ends[2] : ends[3]], kv_total], axis=1),
        middle_total[:, ends[0] : ends[1]],
        gain_own[1],
        middle_total[:, : ends[0]],
        unfold(middle_total[:, ends[1] : ends[2]]),
    )


def solution(mesh):
    return jax.shard_map(
        on_device,
        mesh=mesh,
        in_specs=(
            P("fsdp", "ctx", None),
            P(),
            P("fsdp"),
            P("fsdp", None),
            P("fsdp", None),
            P("fsdp"),
            P("fsdp", None),
            P("fsdp", None),
            P("fsdp", "ctx", None),
        ),
        out_specs=(
            P("fsdp", "ctx", None),
            P("fsdp", "ctx", None),
            P("fsdp"),
            P("fsdp", None),
            P("fsdp", None),
            P("fsdp"),
            P("fsdp", None),
            P("fsdp", None),
        ),
        check_vma=False,
    )
```

time: 998 us -> 448 us (0.45)
  waiting for transfers between devices: 463 us -> 177 us
  blocking collectives: 214 us -> 40.2 us
  local copies, waits for them, and re-layouts: 128 us -> 16.2 us
  starting transfers between devices: 0.69 us -> 107 us
  matrix products: 111 us -> 12.3 us
  Pallas kernels: 0 us -> 63.5 us
  other arithmetic: 52.7 us -> 24.9 us
  between operations: 18.4 us -> 2.52 us
    reduce_scatter x6 -> x0, waiting for transfers between devices: 348 us -> none  [the longest x1 120 us: on_device(): lax.psum_scatter(keys_home, 'ctx', scatter_dimension=0, tiled=True)]
    ppermute x0 -> x108, waiting for transfers between devices: none -> 177 us  [the longest x84 100 us: shift(): return lax.ppermute(array, 'ctx', pairs)]
    psum x1, blocking collectives: 200 us -> 40.2 us  [on_device(): lax.psum(jnp.stack([grad_gain_one[0], grad_gain_two]), ('ctx', 'fsdp'))]
    all_gather x6 -> x0, waiting for transfers between devices: 113 us -> none  [the longest x1 59.2 us: on_device(): all_keys = lax.all_gather(keys_rot, 'ctx', axis=0, tiled=True)]
    ppermute x0 -> x108, starting transfers between devices: none -> 107 us  [the longest x84 92.9 us: shift(): return lax.ppermute(array, 'ctx', pairs)]
    dot_general x48 -> x9, matrix products: 111 us -> 12.3 us  [the longest x6 8.03 us: dot(): lax.dot_general(left, right, (((left_dim,), (right_dim,)), ((), ())), pre...]
    pallas_call x0 -> x6, Pallas kernels: none -> 63.5 us  [the longest x1 27.8 us: attend_back(): pl.pallas_call(partial(attend_back_kernel, groups, per), grid=(PAIRS,), i...]
    another operation x7 -> x4, local copies, waits for them, and re-layouts: 26.2 us -> 1.33 us  [on_device(): jnp.stack([norm_one, norm_two]).astype(f32)]
  transfers between devices with their start and end apart: 12 -> 108, of which waited for: 9 -> 48; matrix products, arithmetic and copies ran while one was open for 14% -> 7% of each run, Pallas kernels for 0% -> 3%
where the time goes in v1:
time: 448 us; the launch traced here: 443 us
  waiting for transfers between devices  177 us (40%)
  starting transfers between devices  107 us (24%)
  Pallas kernels  63.5 us (14%)
  blocking collectives  40.2 us (9%)
  other arithmetic  24.9 us (6%)
  local copies, waits for them, and re-layouts  16.2 us (4%)
  matrix products  12.3 us (3%)
    ppermute x84, waiting for transfers between devices, shift(): return lax.ppermute(array, 'ctx', pairs)  100 us
    ppermute x84, starting transfers between devices, shift(): return lax.ppermute(array, 'ctx', pairs)  92.9 us
    ppermute x24, waiting for transfers between devices, swap(): return lax.ppermute(array, 'fsdp', [(i, i ^ mask) for i in range(4)])  76.6 us
    psum x1, blocking collectives, on_device(): lax.psum(jnp.stack([grad_gain_one[0], grad_gain_two]), ('ctx', 'fsdp'))  40.2 us
    pallas_call x1, Pallas kernels, attend_back(): pl.pallas_call(partial(attend_back_kernel, groups, per), grid=(PAIRS,), i...  27.8 us
    pallas_call x1, Pallas kernels, attend(): pl.pallas_call(partial(attend_kernel, groups, per), grid=(PAIRS,), in_spe...  17.2 us
    ppermute x24, starting transfers between devices, swap(): return lax.ppermute(array, 'fsdp', [(i, i ^ mask) for i in range(4)])  14 us
    select_n x4, other arithmetic, in_order(): first = [jnp.where(high, b, a) for a, b in zip(low_pair, high_pair)]  9.46 us
  transfers between devices with their start and end apart: 108, of which 48 were waited for; matrix products, arithmetic and copies ran while one was open for 7% of the time, Pallas kernels for 3%

profile of v1, /device:TPU:0, one launch (start us, length us, event | category | flops | bytes accessed | tf_op | source)
XLA Modules:
  0.0 443.1 jit_solution(14803227078694329711)
XLA Ops:
  10.1 8.9 %collective-permute-done.1 = f32[2,192]{1,0:T(2,128)S(1)} collective-permute-done((f32[2,192]{1,0:T(2,128)S(1)}, f32[2,192]{1,0:T(2,128)S(1)}, u32[]{:S(2)}, u32[]{:S(2)}) %collective-permute-start.1) | collective-permute-done | bytes 1568 | tf_op jit(solution)/shard_map/ppermute | solution.py:130
  26.1 14.4 %collective-permute-done.23 = bf16[192,768]{1,0:T(8,128)(2,1)} collective-permute-done((bf16[192,768]{1,0:T(8,128)(2,1)}, bf16[192,768]{1,0:T(8,128)(2,1)}, u32[]{:S(2)}, u32[]{:S(2)}) %collective-permute-start.23) | collective-permute-done | bytes 294944 | tf_op jit(solution)/shard_map/ppermute | solution.py:130
  45.6 4.4 project_kv.1
  52.0 10.1 %collective-permute-done.26 = bf16[192,2304]{1,0:T(8,128)(2,1)} collective-permute-done((bf16[192,2304]{1,0:T(8,128)(2,1)}, bf16[192,2304]{1,0:T(8,128)(2,1)}, u32[]{:S(2)}, u32[]{:S(2)}) %collective-permute-start.26) | collective-permute-done | bytes 884768 | tf_op jit(solution)/shard_map/ppermute | solution.py:130
  67.0 7.5 %collective-permute-done.10 = bf16[256,768]{1,0:T(8,128)(2,1)} collective-permute-done((bf16[256,768]{1,0:T(8,128)(2,1)}, bf16[256,768]{1,0:T(8,128)(2,1)}, u32[]{:S(2)}, u32[]{:S(2)}) %collective-permute-start.10) | collective-permute-done | bytes 393248 | tf_op jit(solution)/shard_map/ppermute | solution.py:54
  76.5 7.9 %collective-permute-done.11 = bf16[256,768]{1,0:T(8,128)(2,1)} collective-permute-done((bf16[256,768]{1,0:T(8,128)(2,1)}, bf16[256,768]{1,0:T(8,128)(2,1)}, u32[]{:S(2)}, u32[]{:S(2)}) %collective-permute-start.11) | collective-permute-done | bytes 393248 | tf_op jit(solution)/shard_map/ppermute | solution.py:54
  96.7 4.4 collective-permute-done.13
  103.4 3.5 broadcast_select_fusion.7
  109.6 5.7 %collective-permute-done.15 = bf16[256,768]{1,0:T(8,128)(2,1)S(1)} collective-permute-done((bf16[256,768]{1,0:T(8,128)(2,1)S(1)}, bf16[256,768]{1,0:T(8,128)(2,1)S(1)}, u32[]{:S(2)}, u32[]{:S(2)}) %collective-permute-start.15) | collective-permute-done | bytes 393248 | tf_op jit(solution)/shard_map/ppermute | solution.py:54
  116.2 17.2 %attend.1 = (bf16[256,768]{1,0:T(8,128)(2,1)}, f32[256,768]{1,0:T(8,128)}, f32[6,2,256,128]{3,2,1,0:T(8,128)}) custom-call(s32[8]{0:T(128)} %copy-done.73, bf16[256,768]{1,0:T(8,128)(2,1)} %copy-done.9, bf16[1,256,768]{2,1,0:T(8,128)(2,1)} %bitcast.7.refs_0_, bf16[1,256,768]{2,1,0:T(8,128)(2,1)} %bitcast.8.refs_1_, bf16[1,256,768]{2,1,0:T(8,128)(2,1)} %bitcast.9.refs_2_, ...), custom_call_target="tpu_custom_call" | custom-call | flops 2415919104 | bytes 6291456 | tf_op jit(solution)/shard_map/attend/pallas_call | solution.py:394
  137.0 3.1 add_convert_fusion.4
  145.5 27.8 %attend_back.1 = (bf16[256,768]{1,0:T(8,128)(2,1)}, bf16[1,256,768]{2,1,0:T(8,128)(2,1)}, bf16[1,256,768]{2,1,0:T(8,128)(2,1)}, bf16[1,256,768]{2,1,0:T(8,128)(2...) custom-call(s32[8]{0:T(128)} %copy-done.73, ...), custom_call_target="tpu_custom_call" | custom-call | flops 4026531840 | bytes 12582912 | tf_op jit(solution)/shard_map/attend_back/pallas_call | solution.py:495
  179.4 4.7 %q_back.1 = (bf16[192,768]{1,0:T(8,128)(2,1)S(1)}, bf16[192,768]{1,0:T(8,128)(2,1)S(1)}, bf16[192,768]{1,0:T(8,128)(2,1)S(1)}, bf16[192,768]{1,0:T(8,128)(2,1)S(1)}, f32[4,256,192]{2,1,0:T(8,128)S(1)}) custom-call(s32[1]{0:T(128)} %bitcast.1.me, bf16[4,256,192]{2,1,0:T(8,128)(2,1)S(1)} %get-tuple-element.42.normed, bf16[256,768]{1,0:T(8,128)(2,1)S(1)} %copy-done.12, ...), custom_call_target="tpu_custom_call" | custom-call | flops 603979776 | bytes 2359296 | tf_op jit(solution)/shard_map/q_back/pallas_call | solution.py:536
  188.9 5.1 %collective-permute-done.39 = bf16[256,768]{1,0:T(8,128)(2,1)S(1)} collective-permute-done((bf16[256,768]{1,0:T(8,128)(2,1)S(1)}, bf16[256,768]{1,0:T(8,128)(2,1)S(1)}, u32[]{:S(2)}, u32[]{:S(2)}) %collective-permute-start.39) | collective-permute-done | bytes 393248 | tf_op jit(solution)/shard_map/ppermute | solution.py:54
  197.3 5.1 %collective-permute-done.33 = bf16[256,768]{1,0:T(8,128)(2,1)S(1)} collective-permute-done((bf16[256,768]{1,0:T(8,128)(2,1)S(1)}, bf16[256,768]{1,0:T(8,128)(2,1)S(1)}, u32[]{:S(2)}, u32[]{:S(2)}) %collective-permute-start.33) | collective-permute-done | bytes 393248 | tf_op jit(solution)/shard_map/ppermute | solution.py:54
  205.7 8.0 %collective-permute-done.43 = bf16[256,768]{1,0:T(8,128)(2,1)S(1)} collective-permute-done((bf16[256,768]{1,0:T(8,128)(2,1)S(1)}, bf16[256,768]{1,0:T(8,128)(2,1)S(1)}, u32[]{:S(2)}, u32[]{:S(2)}) %collective-permute-start.43) | collective-permute-done | bytes 393248 | tf_op jit(solution)/shard_map/ppermute | solution.py:54
  216.1 3.2 collective-permute-done.34
  221.2 6.4 %collective-permute-done.44 = bf16[256,768]{1,0:T(8,128)(2,1)S(1)} collective-permute-done((bf16[256,768]{1,0:T(8,128)(2,1)S(1)}, bf16[256,768]{1,0:T(8,128)(2,1)S(1)}, u32[]{:S(2)}, u32[]{:S(2)}) %collective-permute-start.44) | collective-permute-done | bytes 393248 | tf_op jit(solution)/shard_map/ppermute | solution.py:54
  232.5 3.1 collective-permute-done.45.v_two
  235.6 6.6 %kv_back.1 = (bf16[192,1536]{1,0:T(8,128)(2,1)S(1)}, bf16[192,1536]{1,0:T(8,128)(2,1)S(1)}, bf16[192,1536]{1,0:T(8,128)(2,1)S(1)}, bf16[192,1536]{1,0:T(8,128)(2...) custom-call(s32[1]{0:T(128)} %bitcast.1.me, bf16[4,256,192]{2,1,0:T(8,128)(2,1)S(1)} %get-tuple-element.42.normed, ...), custom_call_target="tpu_custom_call" | custom-call | flops 1207959552 | bytes 4718592 | tf_op jit(solution)/shard_map/kv_back/pallas_call | solution.py:608
  250.0 10.8 %collective-permute-done.79 = bf16[192,1536]{1,0:T(8,128)(2,1)S(1)} collective-permute-done((bf16[192,1536]{1,0:T(8,128)(2,1)S(1)}, bf16[192,1536]{1,0:T(8,128)(2,1)S(1)}, u32[]{:S(2)}, u32[]{:S(2)}) %collective-permute-start.79) | collective-permute-done | bytes 589856 | tf_op jit(solution)/shard_map/ppermute | solution.py:130
  284.0 40.2 %psum.7 = f32[2,768]{1,0:T(2,128)S(1)} all-reduce(f32[2,768]{1,0:T(2,128)S(1)} %pad_maximum_fusion.32), channel_id=1, replica_groups=mesh['ctx'=8,'fsdp'=4] {'ctx','fsdp'}, use_global_device_ids=true, to_apply=%region_6.7 | all-reduce | flops 1536 | bytes 12288 | tf_op jit(solution)/shard_map/psum | solution.py:758
  354.1 29.3 %collective-permute-done.48 = bf16[192,4992]{1,0:T(8,128)(2,1)S(1)} collective-permute-done((bf16[192,4992]{1,0:T(8,128)(2,1)S(1)}, bf16[192,4992]{1,0:T(8,128)(2,1)S(1)}, u32[]{:S(2)}, u32[]{:S(2)}) %collective-permute-start.48) | collective-permute-done | bytes 1916960 | tf_op jit(solution)/shard_map/ppermute | solution.py:130
  434.1 3.5 collective-permute-done.72
  (477 shorter events, 199.7 us)
Async XLA Ops:
  1.9 17.7 %collective-permute-start.4 = (bf16[192,1536]{1,0:T(8,128)(2,1)S(1)}, bf16[192,1536]{1,0:T(8,128)(2,1)S(1)}, u32[]{:S(2)}, u32[]{:S(2)}) collective-permute-start(bf16[192,1536]{1,0:T(8,128)(2,1)S(1)} %slice.201.w0), channel_id=1, source_target_pairs={{0,2},{1,3},{2,0},{3,1},{4,6},{5,7},{6,4},{7,5},{8,10},{9,11},{10,... | collective-permute-start | bytes 1769480 | tf_op jit(solution)/shard_map/ppermute | solution.py:130
  7.9 16.9 %collective-permute-start.7 = (bf16[192,768]{1,0:T(8,128)(2,1)S(1)}, bf16[192,768]{1,0:T(8,128)(2,1)}, u32[]{:S(2)}, u32[]{:S(2)}) collective-permute-start(bf16[192,768]{1,0:T(8,128)(2,1)S(1)} %slice.203.w0), channel_id=1, source_target_pairs={{0,2},{1,3},{2,0},{3,1},{4,6},{5,7},{6,4},{7,5},{8,10},{9,11},{10,... | collective-permute-start | bytes 884744 | tf_op jit(solution)/shard_map/ppermute | solution.py:130
  19.1 23.9 %collective-permute-start.3 = (bf16[192,1536]{1,0:T(8,128)(2,1)S(1)}, bf16[192,1536]{1,0:T(8,128)(2,1)S(1)}, u32[]{:S(2)}, u32[]{:S(2)}) collective-permute-start(bf16[192,1536]{1,0:T(8,128)(2,1)S(1)} %slice.201.w0), channel_id=1, source_target_pairs={{0,1},{1,0},{2,3},{3,2},{4,5},{5,4},{6,7},{7,6},{8,9},{9,8},{10,11... | collective-permute-start | bytes 1769480 | tf_op jit(solution)/shard_map/ppermute | solution.py:130
  19.6 23.5 %collective-permute-start.5 = (bf16[192,1536]{1,0:T(8,128)(2,1)S(1)}, bf16[192,1536]{1,0:T(8,128)(2,1)S(1)}, u32[]{:S(2)}, u32[]{:S(2)}) collective-permute-start(bf16[192,1536]{1,0:T(8,128)(2,1)S(1)} %collective-permute-done.4.w2), channel_id=1, source_target_pairs={{0,1},{1,0},{2,3},{3,2},{4,5},{5,4},{6,7},{7,6},{8,9},{9,8},{10,11... | collective-permute-start | bytes 1769480 | tf_op jit(solution)/shard_map/ppermute | solution.py:130
  21.1 21.1 %collective-permute-start.29 = (bf16[288,768]{1,0:T(8,128)(2,1)}, bf16[288,768]{1,0:T(8,128)(2,1)}, u32[]{:S(2)}, u32[]{:S(2)}) collective-permute-start(bf16[288,768]{1,0:T(8,128)(2,1)} %param.17), channel_id=1, source_target_pairs={{0,2},{1,3},{2,0},{3,1},{4,6},{5,7},{6,4},{7,5},{8,10},{9,11},{10,... | collective-permute-start | bytes 1327112 | tf_op jit(solution)/shard_map/ppermute | solution.py:130
  23.1 17.3 %collective-permute-start.23 = (bf16[192,768]{1,0:T(8,128)(2,1)}, bf16[192,768]{1,0:T(8,128)(2,1)}, u32[]{:S(2)}, u32[]{:S(2)}) collective-permute-start(bf16[192,768]{1,0:T(8,128)(2,1)} %param.14), channel_id=1, source_target_pairs={{0,2},{1,3},{2,0},{3,1},{4,6},{5,7},{6,4},{7,5},{8,10},{9,11},{10,... | collective-permute-start | bytes 884744 | tf_op jit(solution)/shard_map/ppermute | solution.py:130
  24.8 17.4 %collective-permute-start.25 = (bf16[192,768]{1,0:T(8,128)(2,1)}, bf16[192,768]{1,0:T(8,128)(2,1)S(1)}, u32[]{:S(2)}, u32[]{:S(2)}) collective-permute-start(bf16[192,768]{1,0:T(8,128)(2,1)} %param.14), channel_id=1, source_target_pairs={{0,1},{1,0},{2,3},{3,2},{4,5},{5,4},{6,7},{7,6},{8,9},{9,8},{10,11... | collective-permute-start | bytes 884744 | tf_op jit(solution)/shard_map/ppermute | solution.py:130
  40.5 21.7 %collective-permute-start.26 = (bf16[192,2304]{1,0:T(8,128)(2,1)}, bf16[192,2304]{1,0:T(8,128)(2,1)}, u32[]{:S(2)}, u32[]{:S(2)}) collective-permute-start(bf16[192,2304]{1,0:T(8,128)(2,1)} %param.16), channel_id=1, source_target_pairs={{0,2},{1,3},{2,0},{3,1},{4,6},{5,7},{6,4},{7,5},{8,10},{9,11},{10,... | collective-permute-start | bytes 2654216 | tf_op jit(solution)/shard_map/ppermute | solution.py:130
  42.2 21.4 %collective-permute-start.28 = (bf16[192,2304]{1,0:T(8,128)(2,1)}, bf16[192,2304]{1,0:T(8,128)(2,1)}, u32[]{:S(2)}, u32[]{:S(2)}) collective-permute-start(bf16[192,2304]{1,0:T(8,128)(2,1)} %param.16), channel_id=1, source_target_pairs={{0,1},{1,0},{2,3},{3,2},{4,5},{5,4},{6,7},{7,6},{8,9},{9,8},{10,11... | collective-permute-start | bytes 2654216 | tf_op jit(solution)/shard_map/ppermute | solution.py:130
  64.1 20.3 %collective-permute-start.11 = (bf16[256,768]{1,0:T(8,128)(2,1)}, bf16[256,768]{1,0:T(8,128)(2,1)}, u32[]{:S(2)}, u32[]{:S(2)}) collective-permute-start(bf16[256,768]{1,0:T(8,128)(2,1)} %collective-permute-done.9), channel_id=1, source_target_pairs={{0,8},{8,16},{16,24},{24,28},{28,20},{20,12},{12,4},{4,0},{1,9},{9... | collective-permute-start | bytes 1179656 | tf_op jit(solution)/shard_map/ppermute | solution.py:54
  65.7 19.2 %collective-permute-start.19 = (bf16[256,768]{1,0:T(8,128)(2,1)}, bf16[256,768]{1,0:T(8,128)(2,1)}, u32[]{:S(2)}, u32[]{:S(2)}) collective-permute-start(bf16[256,768]{1,0:T(8,128)(2,1)} %collective-permute-done.17), channel_id=1, source_target_pairs={{0,4},{8,0},{16,8},{24,16},{28,24},{20,28},{12,20},{4,12},{1,5},{9... | collective-permute-start | bytes 1179656 | tf_op jit(solution)/shard_map/ppermute | solution.py:54
  66.2 37.2 %collective-permute-start.27 = (bf16[192,2304]{1,0:T(8,128)(2,1)}, bf16[192,2304]{1,0:T(8,128)(2,1)S(1)}, u32[]{:S(2)}, u32[]{:S(2)}) collective-permute-start(bf16[192,2304]{1,0:T(8,128)(2,1)} %collective-permute-done.26), channel_id=1, source_target_pairs={{0,1},{1,0},{2,3},{3,2},{4,5},{5,4},{6,7},{7,6},{8,9},{9,8},{10,11... | collective-permute-start | bytes 2654216 | tf_op jit(solution)/shard_map/ppermute | solution.py:130
  74.5 20.2 %collective-permute-start.12 = (bf16[256,768]{1,0:T(8,128)(2,1)}, bf16[256,768]{1,0:T(8,128)(2,1)S(1)}, u32[]{:S(2)}, u32[]{:S(2)}) collective-permute-start(bf16[256,768]{1,0:T(8,128)(2,1)} %collective-permute-done.10), channel_id=1, source_target_pairs={{0,4},{8,0},{16,8},{24,16},{28,24},{20,28},{12,20},{4,12},{1,5},{9... | collective-permute-start | bytes 1179656 | tf_op jit(solution)/shard_map/ppermute | solution.py:54
  76.0 20.3 %collective-permute-start.18 = (bf16[256,768]{1,0:T(8,128)(2,1)}, bf16[256,768]{1,0:T(8,128)(2,1)S(1)}, u32[]{:S(2)}, u32[]{:S(2)}) collective-permute-start(bf16[256,768]{1,0:T(8,128)(2,1)} %collective-permute-done.16), channel_id=1, source_target_pairs={{0,8},{8,16},{16,24},{24,28},{28,20},{20,12},{12,4},{4,0},{1,9},{9... | collective-permute-start | bytes 1179656 | tf_op jit(solution)/shard_map/ppermute | solution.py:54
  176.7 17.3 %collective-permute-start.39 = (bf16[256,768]{1,0:T(8,128)(2,1)S(1)}, bf16[256,768]{1,0:T(8,128)(2,1)S(1)}, u32[]{:S(2)}, u32[]{:S(2)}) collective-permute-start(bf16[256,768]{1,0:T(8,128)(2,1)S(1)} %bitcast.118), channel_id=1, source_target_pairs={{0,4},{8,0},{16,8},{24,16},{28,24},{20,28},{12,20},{4,12},{1,5},{9... | collective-permute-start | bytes 1179656 | tf_op jit(solution)/shard_map/ppermute | solution.py:54
  178.4 18.4 %collective-permute-start.42 = (bf16[256,768]{1,0:T(8,128)(2,1)S(1)}, bf16[256,768]{1,0:T(8,128)(2,1)S(1)}, u32[]{:S(2)}, u32[]{:S(2)}) collective-permute-start(bf16[256,768]{1,0:T(8,128)(2,1)S(1)} %bitcast.117), channel_id=1, source_target_pairs={{0,8},{8,16},{16,24},{24,28},{28,20},{20,12},{12,4},{4,0},{1,9},{9... | collective-permute-start | bytes 1179656 | tf_op jit(solution)/shard_map/ppermute | solution.py:54
  188.5 16.8 %collective-permute-start.37 = (bf16[256,768]{1,0:T(8,128)(2,1)S(1)}, bf16[256,768]{1,0:T(8,128)(2,1)S(1)}, u32[]{:S(2)}, u32[]{:S(2)}) collective-permute-start(bf16[256,768]{1,0:T(8,128)(2,1)S(1)} %fusion.14), channel_id=1, source_target_pairs={{0,8},{8,16},{16,24},{24,28},{28,20},{20,12},{12,4},{4,0},{1,9},{9... | collective-permute-start | bytes 1179656 | tf_op jit(solution)/shard_map/ppermute | solution.py:54
  194.1 20.1 %collective-permute-start.40 = (bf16[256,768]{1,0:T(8,128)(2,1)S(1)}, bf16[256,768]{1,0:T(8,128)(2,1)S(1)}, u32[]{:S(2)}, u32[]{:S(2)}) collective-permute-start(bf16[256,768]{1,0:T(8,128)(2,1)S(1)} %fusion.12), channel_id=1, source_target_pairs={{0,4},{8,0},{16,8},{24,16},{28,24},{20,28},{12,20},{4,12},{1,5},{9... | collective-permute-start | bytes 1179656 | tf_op jit(solution)/shard_map/ppermute | solution.py:54
  205.4 24.2 %collective-permute-start.38 = (bf16[256,768]{1,0:T(8,128)(2,1)S(1)}, bf16[256,768]{1,0:T(8,128)(2,1)S(1)}, u32[]{:S(2)}, u32[]{:S(2)}) collective-permute-start(bf16[256,768]{1,0:T(8,128)(2,1)S(1)} %fusion.15), channel_id=1, source_target_pairs={{0,8},{8,16},{16,24},{24,28},{28,20},{20,12},{12,4},{4,0},{1,9},{9... | collective-permute-start | bytes 1179656 | tf_op jit(solution)/shard_map/ppermute | solution.py:54
  248.4 84.4 %collective-permute-start.47 = (bf16[192,4992]{1,0:T(8,128)(2,1)}, bf16[192,4992]{1,0:T(8,128)(2,1)S(1)}, u32[]{:S(2)}, u32[]{:S(2)}) collective-permute-start(bf16[192,4992]{1,0:T(8,128)(2,1)} %constant_dynamic-update-slice_fusion.3), channel_id=1, source_target_pairs={{0,1},{1,0},{2,3},{3,2},{4,5},{5,4},{6,7},{7,6},{8,9},{9,8},{10,11... | collective-permute-start | bytes 5750792 | tf_op jit(solution)/shard_map/ppermute | solution.py:130
  279.4 74.7 %collective-permute-start.46 = (bf16[192,4992]{1,0:T(8,128)(2,1)}, bf16[192,4992]{1,0:T(8,128)(2,1)}, u32[]{:S(2)}, u32[]{:S(2)}) collective-permute-start(bf16[192,4992]{1,0:T(8,128)(2,1)} %constant_dynamic-update-slice_fusion.1), channel_id=1, source_target_pairs={{0,1},{1,0},{2,3},{3,2},{4,5},{5,4},{6,7},{7,6},{8,9},{9,8},{10,11... | collective-permute-start | bytes 5750792 | tf_op jit(solution)/shard_map/ppermute | solution.py:130
  282.0 44.5 %collective-permute-start.88 = (bf16[24,768]{1,0:T(8,128)(2,1)S(1)}, bf16[24,768]{1,0:T(8,128)(2,1)S(1)}, u32[]{:S(2)}, u32[]{:S(2)}) collective-permute-start(bf16[24,768]{1,0:T(8,128)(2,1)S(1)} %get-tuple-element.131), channel_id=1, source_target_pairs={{0,4},{8,0},{16,8},{24,16},{28,24},{20,28},{12,20},{4,12},{1,5},{9... | collective-permute-start | bytes 110600 | tf_op jit(solution)/shard_map/ppermute | solution.py:54
  283.2 43.3 %collective-permute-start.91 = (bf16[24,768]{1,0:T(8,128)(2,1)S(1)}, bf16[24,768]{1,0:T(8,128)(2,1)S(1)}, u32[]{:S(2)}, u32[]{:S(2)}) collective-permute-start(bf16[24,768]{1,0:T(8,128)(2,1)S(1)} %get-tuple-element.130), channel_id=1, source_target_pairs={{0,8},{8,16},{16,24},{24,28},{28,20},{20,12},{12,4},{4,0},{1,9},{9... | collective-permute-start | bytes 110600 | tf_op jit(solution)/shard_map/ppermute | solution.py:54
  347.3 36.1 %collective-permute-start.48 = (bf16[192,4992]{1,0:T(8,128)(2,1)S(1)}, bf16[192,4992]{1,0:T(8,128)(2,1)S(1)}, u32[]{:S(2)}, u32[]{:S(2)}) collective-permute-start(bf16[192,4992]{1,0:T(8,128)(2,1)S(1)} %add_convert_fusion.1), channel_id=1, source_target_pairs={{0,2},{1,3},{2,0},{3,1},{4,6},{5,7},{6,4},{7,5},{8,10},{9,11},{10,... | collective-permute-start | bytes 5750792 | tf_op jit(solution)/shard_map/ppermute | solution.py:130
  (159 other events, 1641.9 us)

commit v2 on v1

v2 whole, which is shorter than its diff:
```python
from functools import partial

import jax
import jax.numpy as jnp
from jax import lax
from jax.experimental import pallas as pl
from jax.experimental.pallas import tpu as pltpu
from jax.sharding import PartitionSpec as P

D = 768
HEAD_DIM = 64
FF = 1152
LANES = 128
PAIRS = D // LANES
COLS = 256
SCALE = HEAD_DIM**-0.5

theta_base = 160000.0
norm_eps = 1e-05
neg_large = -1e30
f32 = jnp.float32
bf16 = jnp.bfloat16

SMEM = pl.BlockSpec(memory_space=pltpu.SMEM)
WHOLE = pl.BlockSpec(memory_space=pltpu.VMEM)


def params(megabytes):
    return pltpu.CompilerParams(vmem_limit_bytes=megabytes * 2**20)


def cost(microseconds):
    return pl.CostEstimate(flops=int(microseconds * 1.15e9), bytes_accessed=1000, transcendentals=0)


def dot(left, right, left_dim, right_dim):
    return lax.dot_general(
        left, right, (((left_dim,), (right_dim,)), ((), ())), preferred_element_type=f32
    )


def ring_device(place, count):
    return jnp.where(place < count // 2, 2 * place, 2 * (count - 1 - place) + 1)


def ring_place(device, count):
    return jnp.where(device % 2 == 0, device // 2, count - 1 - device // 2)


def shift(array, step, count):
    half = count // 2
    order = [2 * i if i < half else 2 * (count - 1 - i) + 1 for i in range(count)]
    pairs = [(order[i], order[(i + step) % count]) for i in range(count)]
    return lax.ppermute(array, "ctx", pairs)


def ring_offsets(count):
    half = count // 2
    offsets = [0]
    for distance in range(1, half):
        offsets += [-distance, distance]
    return offsets + [half]


def ring_gather(first, second, count):
    half = count // 2
    firsts, seconds = [first], [second]
    up, down = (first, second), (first, second)
    for _ in range(1, half):
        up = tuple(shift(part, 1, count) for part in up)
        down = tuple(shift(part, -1, count) for part in down)
        firsts += [up[0], down[0]]
        seconds += [up[1], down[1]]
    firsts.append(shift(up[0], 1, count))
    seconds.append(shift(down[1], -1, count))
    return firsts, seconds


def add_rounded(left, right):
    return (left.astype(f32) + right.astype(f32)).astype(bf16)


class RingTotal:
    def __init__(self, rows, count):
        self.rows, self.count = rows, count
        self.half = count // 2
        self.place = ring_place(lax.axis_index("ctx"), count)
        self.part = rows.shape[0] // count
        self.fits = rows.shape[0] % (8 * count) == 0
        self.hops = 2 * self.half if self.fits else 0
        self.done = 0
        self.up = self.down = None
        self.parts = [None] * count
        if not self.fits:
            self.total = lax.psum(rows, "ctx")

    def piece(self, offset):
        start = ((self.place + offset) % self.count) * self.part
        return lax.dynamic_slice_in_dim(self.rows, start, self.part, 0)

    def state(self):
        return [array for array in (self.up, self.down) if array is not None]

    def hop(self, earlier=()):
        if self.done >= self.hops:
            return
        self.done += 1
        if self.done <= self.half:
            distance = self.half + 1 - self.done
            down = self.piece(-distance)
            down = down if self.down is None else add_rounded(down, self.down)
            up = None
            if distance < self.half:
                up = self.piece(distance)
                up = up if self.up is None else add_rounded(up, self.up)
        else:
            if self.done == self.half + 1:
                own = self.piece(0).astype(f32) + self.down.astype(f32) + self.up.astype(f32)
                self.up = self.down = self.parts[0] = own.astype(bf16)
            distance = self.done - self.half
            up, down = self.up, (self.down if distance < self.half else None)
            if distance == self.half:
                self.down = None
        if earlier:
            up, down, _ = lax.optimization_barrier((up, down, earlier))
        if self.done <= self.half:
            self.down = shift(down, -1, self.count)
            if up is not None:
                self.up = shift(up, 1, self.count)
        else:
            self.up = self.parts[self.count - distance] = shift(up, 1, self.count)
            if down is not None:
                self.down = self.parts[distance] = shift(down, -1, self.count)

    def columns(self, columns):
        if not self.fits:
            return self.total[:, columns].astype(f32)
        line = [one[:, columns] for one in self.parts]
        twice = jnp.concatenate(line + line, axis=0)
        start = ((self.count - self.place) % self.count) * self.part
        return lax.dynamic_slice_in_dim(twice, start, self.rows.shape[0], 0).astype(f32)


def swap(array, mask):
    return lax.ppermute(array, "fsdp", [(i, i ^ mask) for i in range(4)])


def gather_pieces(piece):
    far = swap(piece, 2)
    return [piece, swap(piece, 1), far, swap(far, 1)]


def core_sums(pieces):
    near, far = swap(pieces[1], 1), swap(pieces[3], 1)
    return (pieces[0], near), add_all([(pieces[2], far)])[0]


def add_all(groups):
    return [sum(part.astype(f32) for part in group).astype(bf16) for group in groups]


def after(array, earlier):
    return lax.optimization_barrier((array, earlier))[0]


def in_order(pieces, me):
    odd = (me % 2) == 1
    high = (me // 2) == 1
    low_pair = [jnp.where(odd, pieces[1], pieces[0]), jnp.where(odd, pieces[0], pieces[1])]
    high_pair = [jnp.where(odd, pieces[3], pieces[2]), jnp.where(odd, pieces[2], pieces[3])]
    first = [jnp.where(high, b, a) for a, b in zip(low_pair, high_pair)]
    last = [jnp.where(high, a, b) for a, b in zip(low_pair, high_pair)]
    return jnp.concatenate(first + last, axis=0)


def out_of_order(whole, me):
    rows = whole.shape[0] // 4
    return [lax.dynamic_slice_in_dim(whole, (me ^ i) * rows, rows, 0) for i in range(4)]


def swap_halves(block):
    lane = lax.broadcasted_iota(jnp.int32, block.shape, 1)
    ahead = pltpu.roll(block, block.shape[1] - HEAD_DIM // 2, 1)
    behind = pltpu.roll(block, HEAD_DIM // 2, 1)
    return jnp.where(lane % HEAD_DIM < HEAD_DIM // 2, ahead, behind)


def normalise(rows):
    mean_value = jnp.mean(rows, axis=-1, keepdims=True)
    centered = rows - mean_value
    spread = jnp.mean(centered * centered, axis=-1, keepdims=True)
    inverse = lax.rsqrt(spread + norm_eps)
    return centered * inverse, inverse


def normed_times(normed, weights, mine):
    total = None
    for i, weight in enumerate(weights):
        part = dot(normed[mine ^ i], weight[: D // 4, :], 1, 0)
        total = part if total is None else total + part
    return total


def rotated(total, cosine, sine, target):
    for i in range(COLS // LANES):
        columns = slice(i * LANES, (i + 1) * LANES)
        block = total[:, columns]
        target[:, columns] = (block * cosine[...] + swap_halves(block) * sine[...]).astype(bf16)


def key_kernel(me, tokens, w0, w1, w2, w3, cosine, sine, keys, normed, gains):
    quarter = D // 4
    mine = me[0]
    weights = (w0, w1, w2, w3)

    @pl.when(pl.program_id(0) == 0)
    def _():
        unit, _ = normalise(tokens[...].astype(f32))
        for i, weight in enumerate(weights):
            gains[mine ^ i] = weight[quarter : quarter + 16, :quarter].astype(f32)[0:1, :]
        for i in range(4):
            normed[i] = (unit[:, i * quarter : (i + 1) * quarter] * gains[i]).astype(bf16)

    rotated(normed_times(normed, weights, mine), cosine, sine, keys)


def fixed(*shape):
    return pl.BlockSpec(shape, lambda j: (0,) * len(shape))


def project_keys(me, tokens, weights, cosine, sine):
    rows = tokens.shape[0]
    return pl.pallas_call(
        key_kernel,
        grid=(D // COLS,),
        in_specs=[SMEM, fixed(rows, D)]
        + [pl.BlockSpec((D // 4 + 16, COLS), lambda j: (0, j))] * 4
        + [fixed(rows, LANES)] * 2,
        out_specs=[
            pl.BlockSpec((rows, COLS), lambda j: (0, j)),
            fixed(4, rows, D // 4),
            fixed(4, 1, D // 4),
        ],
        out_shape=[
            jax.ShapeDtypeStruct((rows, D), bf16),
            jax.ShapeDtypeStruct((4, rows, D // 4), bf16),
            jax.ShapeDtypeStruct((4, 1, D // 4), f32),
        ],
        compiler_params=params(32),
        cost_estimate=cost(2),
        name="project_keys",
    )(me, tokens, *weights, cosine, sine)


def query_kernel(me, normed, w0, w1, w2, w3, cosine, sine, queries):
    rotated(normed_times(normed, (w0, w1, w2, w3), me[0]), cosine, sine, queries)


def value_kernel(me, normed, w0, w1, w2, w3, values):
    values[...] = normed_times(normed, (w0, w1, w2, w3), me[0]).astype(bf16)


def project(me, normed, weights, tables=()):
    rows = normed.shape[1]
    return pl.pallas_call(
        query_kernel if tables else value_kernel,
        grid=(D // COLS,),
        in_specs=[SMEM, fixed(4, rows, D // 4)]
        + [pl.BlockSpec((D // 4, COLS), lambda j: (0, j))] * 4
        + [fixed(rows, LANES)] * len(tables),
        out_specs=pl.BlockSpec((rows, COLS), lambda j: (0, j)),
        out_shape=jax.ShapeDtypeStruct((rows, D), bf16),
        compiler_params=params(32),
        cost_estimate=cost(2),
        name="project_queries" if tables else "project_values",
    )(me, normed, *weights, *tables)


def stacked(block, factor=None):
    if factor is not None:
        block = block * jnp.asarray(factor, block.dtype)
    lane = lax.broadcasted_iota(jnp.int32, block.shape, 1)
    zero = jnp.zeros_like(block)
    return jnp.concatenate(
        [jnp.where(lane < HEAD_DIM, block, zero), jnp.where(lane < HEAD_DIM, zero, block)], axis=0
    )


def unstacked(block):
    rows = block.shape[0] // 2
    lane = lax.broadcasted_iota(jnp.int32, (rows, block.shape[1]), 1)
    return jnp.where(lane < HEAD_DIM, block[:rows], block[rows:])


def causal(scores):
    rows, columns = scores.shape
    row = lax.broadcasted_iota(jnp.int32, scores.shape, 0) % (rows // 2)
    column = lax.broadcasted_iota(jnp.int32, scores.shape, 1)
    return jnp.where(column <= row, scores, neg_large)


def over_chunks(groups, per, first, visit, carry):
    for group in range(groups):
        start = first if group == 0 else 0
        if per == 1:
            if start == 0:
                carry = visit(group, 0, group, carry)
        else:

            def turn(i, held, group=group):
                return visit(group, i, group * per + i, held)

            carry = lax.fori_loop(start, per, turn, carry)
    return carry


def by_head(stacked_column):
    return unstacked(jnp.broadcast_to(stacked_column, (stacked_column.shape[0], LANES)))


def of_heads(block):
    shape = block.shape
    return jnp.concatenate(
        [
            jnp.broadcast_to(block[:, :1], shape),
            jnp.broadcast_to(block[:, HEAD_DIM : HEAD_DIM + 1], shape),
        ],
        axis=0,
    )


def attend_kernel(groups, per, base, merge, blocks, queries, *refs):
    keys, values = refs[:groups], refs[groups : 2 * groups]
    rest = refs[2 * groups :]
    before, rest = (rest[:4], rest[4:]) if merge else ((), rest)
    results, (stack, scores) = rest[:-2], rest[-2:]
    width = queries.shape[0] // 2
    own = blocks[0]
    low, high = slice(0, width), slice(width, 2 * width)
    with_own = base == 0
    empty = jnp.full((2 * width, LANES), neg_large, f32)
    nothing = jnp.zeros((2 * width, LANES), f32)

    def picked(chunk):
        up = blocks[base + chunk] > own
        which = up.astype(jnp.int32)
        return up, which, pl.ds(pl.multiple_of(which * width, width), width)

    for i, rows in enumerate((low, high)):
        stack[i] = stacked(queries[rows, :], SCALE)

    tops = (empty, empty)
    if with_own:
        first = causal(dot(stack[0], keys[0][0, low, :], 1, 1))
        second = causal(dot(stack[1], keys[0][0, high, :], 1, 1))
        third = dot(stack[1], keys[0][0, low, :], 1, 1)
        scores[0], scores[1], scores[2] = first, second, third
        tops = (first, jnp.maximum(second, third))

    def score(group, i, chunk, held):
        up, which, rows = picked(chunk)
        full = dot(stack[1], keys[group][i, low, :], 1, 1)
        part = dot(stack[which], keys[group][i, rows, :], 1, 1)
        scores[2 * chunk + 1] = full
        scores[2 * chunk + 2] = part
        return (
            jnp.maximum(held[0], jnp.where(up, empty, part)),
            jnp.maximum(jnp.maximum(held[1], full), jnp.where(up, part, empty)),
        )

    tops = over_chunks(groups, per, int(with_own), score, tops)
    top_low, top_high = (jnp.max(top, axis=1, keepdims=True) for top in tops)

    def weigh(slot, top, value_rows):
        weight = jnp.exp(scores[slot] - top)
        coarse = weight.astype(bf16)
        fine = (weight - coarse.astype(f32)).astype(bf16)
        return (
            weight,
            unstacked(dot(coarse, value_rows, 1, 0)),
            unstacked(dot(fine, value_rows, 1, 0)),
        )

    def summed(*parts):
        return tuple(sum(terms[1:], terms[0]) for terms in zip(*parts))

    none = (nothing, nothing[low], nothing[low])
    sums = (none, none)
    if with_own:
        sums = (
            weigh(0, top_low, values[0][0, low, :]),
            summed(
                weigh(1, top_high, values[0][0, high, :]), weigh(2, top_high, values[0][0, low, :])
            ),
        )

    def collect(group, i, chunk, held):
        up, which, rows = picked(chunk)
        full = weigh(2 * chunk + 1, top_high, values[group][i, low, :])
        part = weigh(
            2 * chunk + 2, jnp.where(up, top_high, top_low), values[group][i, rows, :]
        )
        to_low = tuple(jnp.where(up, jnp.zeros_like(term), term) for term in part)
        to_high = tuple(jnp.where(up, term, jnp.zeros_like(term)) for term in part)
        return summed(held[0], to_low), summed(held[1], full, to_high)

    sums = over_chunks(groups, per, int(with_own), collect, sums)
    for rows, top, (weight, coarse, fine) in zip((low, high), (top_low, top_high), sums):
        top = by_head(top)
        total = by_head(jnp.sum(weight, axis=1, keepdims=True))
        exact = coarse + fine
        if merge:
            old_top, old_total, old_coarse, old_exact = (ref[rows, :] for ref in before)
            new_top = jnp.maximum(top, old_top)
            now, then = jnp.exp(top - new_top), jnp.exp(old_top - new_top)
            total = total * now + old_total * then
            inverse = 1.0 / total
            attended, exact_out, log_total = results
            attended[rows, :] = ((coarse * now + old_coarse * then) * inverse).astype(bf16)
            exact_out[rows, :] = (exact * now + old_exact * then) * inverse
            log_total[rows, :] = new_top + jnp.log(total)
        else:
            for ref, value in zip(results, (top, total, coarse, exact)):
                ref[rows, :] = value


def grouped(chunks):
    per = 1 if len(chunks) <= 8 else len(chunks) // 4
    if per == 1:
        return [chunk[None] for chunk in chunks]
    return [jnp.stack(chunks[i : i + per]) for i in range(0, len(chunks), per)]


def column_block(rows):
    return pl.BlockSpec((rows, LANES), lambda j: (0, j))


def attend(base, blocks, queries, key_chunks, value_chunks, before=()):
    rows = queries.shape[0]
    keys, values = grouped(key_chunks), grouped(value_chunks)
    groups, per, count = len(keys), keys[0].shape[0], len(key_chunks)
    column = column_block(rows)
    chunk = pl.BlockSpec((per, rows, LANES), lambda j: (0, 0, j))
    types = (bf16, f32, f32) if before else (f32,) * 4
    return pl.pallas_call(
        partial(attend_kernel, groups, per, base, bool(before)),
        grid=(PAIRS,),
        in_specs=[SMEM, column] + [chunk] * (2 * groups) + [column] * len(before),
        out_specs=[column] * len(types),
        out_shape=[jax.ShapeDtypeStruct((rows, D), kind) for kind in types],
        scratch_shapes=[
            pltpu.VMEM((2, rows, LANES), bf16),
            pltpu.VMEM((2 * count + 1, rows, LANES), f32),
        ],
        compiler_params=params(56),
        cost_estimate=cost(2 * count),
        name=f"attend_{base}",
    )(blocks, queries, *keys, *values, *before)


def attend_back_kernel(groups, per, base, carried, blocks, queries, grads, exact, log_total, *refs):
    keys, values = refs[:groups], refs[groups : 2 * groups]
    rest = refs[2 * groups :]
    before, rest = (rest[:1], rest[1:]) if carried else ((), rest)
    with_own = base == 0
    (cosine, sine), rest = (rest[:2], rest[2:]) if with_own else ((None, None), rest)
    grad_queries = rest[0]
    grad_keys = rest[1 : groups + 1]
    grad_values = rest[groups + 1 : 2 * groups + 1]
    stack, grad_stack, deltas, logs = rest[2 * groups + 1 :]
    width = queries.shape[0] // 2
    own = blocks[0]
    low, high = slice(0, width), slice(width, 2 * width)

    for i, rows in enumerate((low, high)):
        stack[i] = stacked(queries[rows, :], SCALE)
        grad_rows = stacked(grads[rows, :])
        grad_stack[i] = grad_rows
        twice = jnp.concatenate([exact[rows, :], exact[rows, :]], axis=0)
        delta = jnp.sum(grad_rows.astype(f32) * twice, axis=1, keepdims=True)
        deltas[i] = jnp.broadcast_to(delta, deltas.shape[1:])
        logs[i] = of_heads(log_total[rows, :])

    def block(which, key_rows, value_rows, diagonal=False):
        query_rows, grad_rows = stack[which], grad_stack[which]
        raw = dot(query_rows, key_rows, 1, 1)
        if diagonal:
            raw = causal(raw)
        probability = jnp.exp(raw - logs[which])
        grad_prob = dot(grad_rows, value_rows, 1, 1)
        grad_scores = (probability * (grad_prob - deltas[which])).astype(bf16)
        return (
            unstacked(dot(grad_scores, key_rows, 1, 0)),
            dot(grad_scores, query_rows, 0, 0),
            dot(probability.astype(bf16), grad_rows, 0, 0),
        )

    if carried:
        sums = (before[0][low, :], before[0][high, :])
    else:
        sums = (jnp.zeros((width, LANES), f32),) * 2
    if with_own:
        key_low, value_low = keys[0][0, low, :], values[0][0, low, :]
        query_one, key_one, value_one = block(0, key_low, value_low, True)
        query_two, key_two, value_two = block(1, keys[0][0, high, :], values[0][0, high, :], True)
        query_all, key_all, value_all = block(1, key_low, value_low)
        sums = (sums[0] + query_one, sums[1] + query_two + query_all)
        grad_keys[0][0, low, :] = (key_one + key_all).astype(bf16)
        grad_values[0][0, low, :] = (value_one + value_all).astype(bf16)
        grad_keys[0][0, high, :] = key_two.astype(bf16)
        grad_values[0][0, high, :] = value_two.astype(bf16)

    def visit(group, i, chunk, held):
        up = blocks[base + chunk] > own
        which = up.astype(jnp.int32)
        rows = pl.ds(pl.multiple_of(which * width, width), width)
        query_all, key_all, value_all = block(1, keys[group][i, low, :], values[group][i, low, :])
        query_one, key_one, value_one = block(
            which, keys[group][i, rows, :], values[group][i, rows, :]
        )
        for target, whole, part in (
            (grad_keys[group], key_all, key_one),
            (grad_values[group], value_all, value_one),
        ):
            zero = jnp.zeros_like(part)
            target[i, low, :] = (whole + jnp.where(up, zero, part)).astype(bf16)
            target[i, high, :] = jnp.where(up, part, zero).astype(bf16)
        zero = jnp.zeros_like(query_one)
        return (
            held[0] + jnp.where(up, zero, query_one),
            held[1] + query_all + jnp.where(up, query_one, zero),
        )

    sums = over_chunks(groups, per, int(with_own), visit, sums)
    for rows, grad in zip((low, high), sums):
        if with_own:
            grad = grad * SCALE
            turned = grad * cosine[rows, :] - swap_halves(grad) * sine[rows, :]
            grad_queries[rows, :] = turned.astype(bf16)
        else:
            grad_queries[rows, :] = grad


def attend_back(base, blocks, queries, grads, exact, log_total, key_chunks, value_chunks, before, tables):
    rows = queries.shape[0]
    keys, values = grouped(key_chunks), grouped(value_chunks)
    groups, per, count = len(keys), keys[0].shape[0], len(key_chunks)
    column = column_block(rows)
    chunk = pl.BlockSpec((per, rows, LANES), lambda j: (0, 0, j))
    stat = pltpu.VMEM((2, rows, LANES), f32)
    half = pltpu.VMEM((2, rows, LANES), bf16)
    extra = (() if before is None else (before,)) + (tuple(tables) if base == 0 else ())
    extra_specs = ([] if before is None else [column]) + ([fixed(rows, LANES)] * 2 if base == 0 else [])
    result = pl.pallas_call(
        partial(attend_back_kernel, groups, per, base, before is not None),
        grid=(PAIRS,),
        in_specs=[SMEM] + [column] * 4 + [chunk] * (2 * groups) + extra_specs,
        out_specs=[column] + [chunk] * (2 * groups),
        out_shape=[jax.ShapeDtypeStruct((rows, D), bf16 if base == 0 else f32)]
        + [jax.ShapeDtypeStruct((per, rows, D), bf16)] * (2 * groups),
        scratch_shapes=[half, half, stat, stat],
        compiler_params=params(56),
        cost_estimate=cost(4.5 * count),
        name=f"attend_back_{base}",
    )(blocks, queries, grads, exact, log_total, *keys, *values, *extra)
    key_grads = [part[i] for part in result[1 : groups + 1] for i in range(per)]
    value_grads = [part[i] for part in result[groups + 1 :] for i in range(per)]
    return result[0], key_grads, value_grads


def q_back_kernel(me, normed, grads, w0, w1, w2, w3, g0, g1, g2, g3, back):
    mine = me[0]
    step = pl.program_id(0)
    block = grads[...]
    for i, (weight, target) in enumerate(((w0, g0), (w1, g1), (w2, g2), (w3, g3))):
        target[...] = dot(normed[mine ^ i], block, 0, 0).astype(bf16)
        part = dot(block, weight[...], 1, 1)

        @pl.when(step == 0)
        def _(i=i, part=part):
            back[mine ^ i] = part

        @pl.when(step > 0)
        def _(i=i, part=part):
            back[mine ^ i] += part


def q_back(me, normed, grads, weights):
    rows = grads.shape[0]

    column = pl.BlockSpec((D // 4, COLS), lambda j: (0, j))
    result = pl.pallas_call(
        q_back_kernel,
        grid=(D // COLS,),
        in_specs=[SMEM, fixed(4, rows, D // 4), pl.BlockSpec((rows, COLS), lambda j: (0, j))]
        + [column] * 4,
        out_specs=[column] * 4 + [fixed(4, rows, D // 4)],
        out_shape=[jax.ShapeDtypeStruct((D // 4, D), bf16)] * 4
        + [jax.ShapeDtypeStruct((4, rows, D // 4), f32)],
        compiler_params=params(32),
        cost_estimate=cost(4),
        name="q_back",
    )(me, normed, grads, *weights)
    return result[:4], result[4]


def middle_grads_kernel(me, normed, grad_gateup, attended, grad_branch, hidden, grad_out, gain, *refs):
    gateups, others = refs[:4], refs[4:8]
    normed_by, attended_by, hidden_by, gain_by = refs[8:]
    mine = me[0]
    quarter, part = D // 4, FF // 4
    ones = jnp.ones((normed.shape[0], LANES), bf16)
    coarse = gain[...].astype(bf16)
    fine = (gain[...] - coarse.astype(f32)).astype(bf16)
    for i in range(4):
        columns = slice(i * quarter, (i + 1) * quarter)
        normed_by[i] = normed[:, columns]
        attended_by[i] = attended[:, columns]
        hidden_by[i] = hidden[:, i * part : (i + 1) * part]
        gain_by[i] = dot(coarse[:, columns], ones, 0, 0) + dot(fine[:, columns], ones, 0, 0)
    for i in (3, 1, 2, 0):
        for first in range(0, 2 * FF, D):
            columns = slice(first, first + D)
            gateups[i][:, columns] = dot(normed_by[mine ^ i], grad_gateup[:, columns], 0, 0).astype(bf16)
        others[i][:, :D] = dot(attended_by[mine ^ i], grad_branch[...], 0, 0).astype(bf16)
        down = dot(hidden_by[mine ^ i], grad_out[...], 0, 0).astype(bf16)
        others[i][:, D : 2 * D] = down[:quarter]
        others[i][: quarter // 2, 2 * D : D + FF] = down[quarter:, : D // 2]
        others[i][quarter // 2 :, 2 * D : D + FF] = down[quarter:, D // 2 :]
        others[i][:, D + FF :] = gain_by[mine ^ i].astype(bf16)


def middle_grads(me, normed, grad_gateup, attended, grad_branch, hidden, grad_out, gain):
    rows = normed.shape[0]
    result = pl.pallas_call(
        middle_grads_kernel,
        in_specs=[SMEM] + [WHOLE] * 7,
        out_specs=[WHOLE] * 8,
        out_shape=[jax.ShapeDtypeStruct((D // 4, 2 * FF), bf16)] * 4
        + [jax.ShapeDtypeStruct((D // 4, D + FF + LANES), bf16)] * 4,
        scratch_shapes=[
            pltpu.VMEM((4, rows, D // 4), bf16),
            pltpu.VMEM((4, rows, D // 4), bf16),
            pltpu.VMEM((4, rows, FF // 4), bf16),
            pltpu.VMEM((4, D // 4, LANES), f32),
        ],
        compiler_params=params(32),
        cost_estimate=cost(4),
        name="middle_grads",
    )(me, normed, grad_gateup, attended, grad_branch, hidden, grad_out, gain)
    return result[:4], result[4:]


def kv_back_kernel(
    me, normed, k_own, k_one, k_two, v_own, v_one, v_two, k0, k1, k2, k3, v0, v1, v2, v3, cosine, sine,
    start, tokens, gains, grad_middle, g0, g1, g2, g3, grad_tokens, back, block_of,
):
    mine = me[0]
    step = pl.program_id(0)
    half = (pl.num_programs(0) - 1) // 2
    quarter = D // 4
    targets = (g0, g1, g2, g3)

    @pl.when(step == 0)
    def _():
        back[...] = start[...]

    @pl.when(step < half)
    def _():
        total = k_own[...].astype(f32) + k_one[...].astype(f32) + k_two[...].astype(f32)
        for i in range(COLS // LANES):
            columns = slice(i * LANES, (i + 1) * LANES)
            part = total[:, columns]
            turned = part * cosine[...] - swap_halves(part) * sine[...]
            block_of[:, columns] = turned.astype(bf16)
        for i, weight in enumerate((k0, k1, k2, k3)):
            targets[i][...] = dot(normed[mine ^ i], block_of[...], 0, 0).astype(bf16)
            back[mine ^ i] += dot(block_of[...], weight[:quarter, :], 1, 1)

    @pl.when((step >= half) & (step < 2 * half))
    def _():
        total = v_own[...].astype(f32) + v_one[...].astype(f32) + v_two[...].astype(f32)
        block = total.astype(bf16)
        for i, weight in enumerate((v0, v1, v2, v3)):
            targets[i][...] = dot(normed[mine ^ i], block, 0, 0).astype(bf16)
            back[mine ^ i] += dot(block, weight[...], 1, 1)

    @pl.when(step == 2 * half)
    def _():
        unit, inverse = normalise(tokens[...].astype(f32))
        ones = jnp.ones((unit.shape[0], COLS), bf16)
        for i in range(4):
            part = back[i] * unit[:, i * quarter : (i + 1) * quarter]
            coarse = part.astype(bf16)
            fine = (part - coarse.astype(f32)).astype(bf16)
            total = (dot(coarse, ones, 0, 0) + dot(fine, ones, 0, 0)).astype(bf16)
            for k in range(4):

                @pl.when((mine ^ k) == i)
                def _(k=k, total=total):
                    targets[k][...] = total

        incoming = jnp.concatenate([back[i] for i in range(4)], axis=1)
        gain = jnp.concatenate([gains[i] for i in range(4)], axis=1)
        scaled = incoming * gain
        mean_one = jnp.mean(scaled, axis=-1, keepdims=True)
        mean_two = jnp.mean(scaled * unit, axis=-1, keepdims=True)
        grad_tokens[...] = grad_middle[...] + inverse * (scaled - mean_one - unit * mean_two)


def kv_back(
    me, normed, key_sums, value_sums, k_weights, v_weights, cosine, sine, start, tokens, gains, grad_middle
):
    rows = tokens.shape[0]
    half = D // COLS

    def early(height):
        return pl.BlockSpec((height, COLS), lambda j: (0, jnp.minimum(j, half - 1)))

    def late(height):
        return pl.BlockSpec((height, COLS), lambda j: (0, jnp.clip(j - half, 0, half - 1)))

    result = pl.pallas_call(
        kv_back_kernel,
        grid=(2 * half + 1,),
        in_specs=[SMEM, fixed(4, rows, D // 4)]
        + [early(rows)] * 3
        + [late(rows)] * 3
        + [early(D // 4 + 16)] * 4
        + [late(D // 4)] * 4
        + [fixed(rows, LANES)] * 2
        + [fixed(4, rows, D // 4), fixed(rows, D), fixed(4, 1, D // 4), fixed(rows, D)],
        out_specs=[pl.BlockSpec((D // 4, COLS), lambda j: (0, j))] * 4 + [fixed(rows, D)],
        out_shape=[jax.ShapeDtypeStruct((D // 4, 2 * D + COLS), bf16)] * 4
        + [jax.ShapeDtypeStruct((rows, D), f32)],
        scratch_shapes=[
            pltpu.VMEM((4, rows, D // 4), f32),
            pltpu.VMEM((rows, COLS), bf16),
        ],
        compiler_params=params(32),
        cost_estimate=cost(8),
        name="kv_back",
    )(
        me, normed, *key_sums, *value_sums, *k_weights, *v_weights, cosine, sine, start, tokens, gains, grad_middle
    )
    return result[:4], result[4]


def layer_norm(token_rows, gain_row):
    mean_value = jnp.mean(token_rows, axis=-1, keepdims=True)
    centered = token_rows - mean_value
    spread = jnp.mean(centered * centered, axis=-1, keepdims=True)
    return centered * lax.rsqrt(spread + norm_eps) * gain_row


def geglu(gate_part, up_part):
    return jax.nn.gelu(gate_part, approximate=False) * up_part


def rope_tables(positions):
    half = HEAD_DIM // 2
    frequency = theta_base ** (-2.0 * jnp.arange(half, dtype=f32) / HEAD_DIM)
    angles = positions.astype(f32)[:, None] * frequency[None, :]
    cosine, sine = jnp.cos(angles), jnp.sin(angles)
    return (
        jnp.concatenate([cosine] * 4, axis=1),
        jnp.concatenate([-sine, sine, -sine, sine], axis=1),
    )


def on_device(
    tokens,
    pair_order,
    norm_one,
    qkv_weight,
    out_weight,
    norm_two,
    gateup_weight,
    down_weight,
    cotangent,
):
    count = lax.axis_size("ctx")
    me = lax.axis_index("fsdp")
    me_row = jnp.reshape(me, (1,)).astype(jnp.int32)
    gain_row = jnp.concatenate(
        [jnp.pad(norm_one, (0, COLS - D // 4)), jnp.pad(norm_two, (0, D - COLS - D // 4))]
    )
    gain_rows = jnp.broadcast_to(gain_row[None, :], (16, D))
    k_weights = gather_pieces(jnp.concatenate([qkv_weight[:, D : 2 * D], gain_rows], axis=0))
    v_weights = gather_pieces(after(qkv_weight[:, 2 * D :], k_weights[2]))
    q_weights = gather_pieces(after(qkv_weight[:, :D], v_weights[2]))
    out_pieces = gather_pieces(after(out_weight, q_weights[2]))
    gateup_pieces = gather_pieces(after(gateup_weight, out_pieces[2]))
    down_pieces = gather_pieces(after(down_weight, gateup_pieces[2]))
    pair_order = after(pair_order, k_weights[1])
    place = ring_place(lax.axis_index("ctx"), count)
    width = tokens.shape[1] // 2
    offsets = jnp.asarray(ring_offsets(count), jnp.int32)
    chunk_devices = ring_device((place + offsets) % count, count)
    blocks = jnp.sum(
        jnp.where(
            chunk_devices[:, None] == jnp.arange(count, dtype=jnp.int32)[None, :],
            pair_order[None, :],
            0,
        ),
        axis=1,
    )
    low_block = blocks[0]
    high_block = 2 * count - 1 - low_block
    within = jnp.arange(width, dtype=jnp.int32)
    positions = jnp.concatenate([low_block * width + within, high_block * width + within])
    cosine, sine = rope_tables(positions)

    token_rows = tokens[0]
    keys, normed, gains = project_keys(me_row, token_rows, k_weights, cosine, sine)
    values = project(me_row, normed, v_weights)
    all_keys, all_values = ring_gather(keys, values, count)
    queries = project(me_row, normed, q_weights, (cosine, sine))
    split = count - 3 if count == 8 else count // 2
    so_far = attend(0, blocks, queries, all_keys[:split], all_values[:split])
    attended, exact, log_total = attend(
        split, blocks, queries, all_keys[split:], all_values[split:], so_far
    )

    weight_out = in_order(out_pieces, me)
    weight_gateup = in_order(gateup_pieces, me)
    weight_down = in_order(down_pieces, me)
    gain_two = in_order([part[D // 4, COLS : COLS + D // 4] for part in k_weights], me).astype(f32)
    middle = token_rows.astype(f32) + jnp.dot(attended, weight_out, preferred_element_type=f32)
    normed_two = layer_norm(middle, gain_two).astype(bf16)
    gateup = jnp.dot(normed_two, weight_gateup, preferred_element_type=f32)
    hidden_f, geglu_pull = jax.vjp(geglu, gateup[:, :FF], gateup[:, FF:])
    hidden = hidden_f.astype(bf16)
    result = middle + jnp.dot(hidden, weight_down, preferred_element_type=f32)
    grad_out = cotangent[0]
    grad_hidden = dot(grad_out, weight_down, 1, 1)
    grad_gate, grad_up = geglu_pull(grad_hidden)
    grad_gateup = jnp.concatenate([grad_gate, grad_up], axis=1).astype(bf16)
    grad_normed_two = dot(grad_gateup, weight_gateup, 1, 1)
    unit_two, inverse_two = normalise(middle)
    scaled = grad_normed_two * gain_two
    mean_one = jnp.mean(scaled, axis=-1, keepdims=True)
    mean_two = jnp.mean(scaled * unit_two, axis=-1, keepdims=True)
    gain_product = grad_normed_two * unit_two
    grad_middle = grad_out.astype(f32) + inverse_two * (scaled - mean_one - unit_two * mean_two)
    grad_branch = grad_middle.astype(bf16)
    grad_attended = dot(grad_branch, weight_out, 1, 1).astype(bf16)

    cuts = [0, 3, 8] if count == 8 else [0, count // 2, count]
    slots = {offset: slot for slot, offset in enumerate(ring_offsets(count))}
    key_parts, value_parts = [None] * count, [None] * count
    grad_queries = None

    def back_part(which, held, earlier):
        first, last = cuts[which], cuts[which + 1]
        query_rows, _ = lax.optimization_barrier((queries, earlier))
        held, key_parts[first:last], value_parts[first:last] = attend_back(
            first, blocks, query_rows, grad_attended, exact, log_total,
            all_keys[first:last], all_values[first:last], held, (cosine, sine),
        )
        return held

    def unfold(piece):
        top, rest = piece[:, :D], piece[:, D:]
        return jnp.concatenate(
            [top, jnp.concatenate([rest[: D // 8], rest[D // 8 :]], axis=1)], axis=0
        )

    def added(parts, which, down, up, distance):
        pair = [parts[slots[-distance]], parts[slots[distance]]]
        groups = [(one, sums[which]) for one, sums in zip(pair, (down, up)) if sums[which] is not None]
        sums = iter(add_all(groups)) if groups else None
        return [
            one if held[which] is None else next(sums) for one, held in zip(pair, (down, up))
        ]

    def hop(down, up, distance):
        arrived = ([], [])
        for which, parts in enumerate((key_parts, value_parts)):
            one, other = added(parts, which, down, up, distance)
            arrived[0].append(shift(one, -1, count))
            arrived[1].append(shift(other, 1, count))
        return arrived

    def mirror(pieces):
        return add_rounded(pieces[2], pieces[3])

    def over_cores(pieces):
        return [pieces[0], swap(pieces[1], 1), pieces[2], swap(pieces[3], 1)]

    def ended(*values):
        return lax.optimization_barrier(values)

    first = cuts[1]
    grad_queries = back_part(1, None, ())
    down = [shift(key_parts[-1], -1, count), None]
    up = [None, shift(value_parts[-1], 1, count)]
    hidden = after(hidden, (key_parts[-1], value_parts[-1]))
    gateup_grads, middle_grads_all = middle_grads(
        me_row, normed_two, grad_gateup, attended, grad_branch, hidden, grad_out, gain_product
    )
    down[0], up[1], gateup_grads, middle_grads_all, grad_queries = ended(
        down[0], up[1], gateup_grads, middle_grads_all, grad_queries
    )
    distances = list(range(count // 2 - 1, 0, -1))
    down, up = hop(down, up, distances[0])
    gateup_grads, middle_grads_all = over_cores(gateup_grads), over_cores(middle_grads_all)
    grad_queries = back_part(0, grad_queries, gateup_grads[0])
    (down, up, gateup_grads, middle_grads_all, grad_queries, key_parts[:first], value_parts[:first]) = ended(
        down, up, gateup_grads, middle_grads_all, grad_queries, key_parts[:first], value_parts[:first]
    )
    down, up = hop(down, up, distances[1])
    gateup_last = swap(mirror(gateup_grads), 2)
    middle_far = mirror(middle_grads_all)
    q_pieces, start = q_back(me_row, normed, grad_queries, q_weights)
    down, up, gateup_last, middle_far, q_pieces, start = ended(
        down, up, gateup_last, middle_far, q_pieces, start
    )
    for distance in distances[2:]:
        down, up = hop(down, up, distance)
    middle_last = swap(middle_far, 2)
    q_pieces = over_cores(q_pieces)
    down, up, middle_last, q_pieces = ended(down, up, middle_last, q_pieces)
    key_sums = (key_parts[0], down[0], up[0])
    value_sums = (value_parts[0], down[1], up[1])
    q_last = swap(mirror(q_pieces), 2)
    kv_pieces, grad_tokens = kv_back(
        me_row, normed, key_sums, value_sums, k_weights, v_weights, cosine, sine, start, token_rows, gains, grad_middle
    )
    gateup_sum, middle_sum = (
        add_all([(pieces[0], pieces[1], last)])[0]
        for pieces, last in ((gateup_grads, gateup_last), (middle_grads_all, middle_last))
    )
    kv_pieces, q_last, gateup_sum, middle_sum = ended(kv_pieces, q_last, gateup_sum, middle_sum)
    q_sum = add_all([(q_pieces[0], q_pieces[1], q_last)])[0]
    middle_total = RingTotal(jnp.concatenate([gateup_sum, middle_sum, q_sum], axis=1), count)
    middle_total.hop()
    kv_pieces = over_cores(kv_pieces)
    kv_pieces, middle_total.up, middle_total.down = ended(
        kv_pieces, middle_total.up, middle_total.down
    )
    kv_last = swap(mirror(kv_pieces), 2)
    middle_total.hop()
    middle_total.hop()
    kv_last, middle_total.up, middle_total.down = ended(
        kv_last, middle_total.up, middle_total.down
    )
    kv_total = RingTotal(add_all([(kv_pieces[0], kv_pieces[1], kv_last)])[0], count)
    while kv_total.done < kv_total.hops - 1:
        kv_total.hop()
        middle_total.hop()
        kv_total.up, kv_total.down, middle_total.up, middle_total.down = ended(
            kv_total.up, kv_total.down, middle_total.up, middle_total.down
        )
    ends = (0, 3 * D, 4 * D, 4 * D + FF, 4 * D + FF + LANES, 5 * D + FF + LANES)
    grad_gateup_weight, grad_out_weight, grad_down, grad_gain, grad_q = (
        middle_total.columns(slice(ends[i], ends[i + 1])) for i in range(5)
    )
    gain_two_own = grad_gain[:, 0]
    grad_down_weight = unfold(grad_down)
    kv_total.hop((grad_gateup_weight, grad_out_weight, grad_down_weight, gain_two_own))
    return (
        result.astype(bf16)[None],
        grad_tokens[None],
        kv_total.columns(slice(2 * D, 2 * D + LANES))[:, 0],
        jnp.concatenate([grad_q, kv_total.columns(slice(0, 2 * D))], axis=1),
        grad_out_weight,
        gain_two_own,
        grad_gateup_weight,
        grad_down_weight,
    )


def solution(mesh):
    return jax.shard_map(
        on_device,
        mesh=mesh,
        in_specs=(
            P("fsdp", "ctx", None),
            P(),
            P("fsdp"),
            P("fsdp", None),
            P("fsdp", None),
            P("fsdp"),
            P("fsdp", None),
            P("fsdp", None),
            P("fsdp", "ctx", None),
        ),
        out_specs=(
            P("fsdp", "ctx", None),
            P("fsdp", "ctx", None),
            P("fsdp"),
            P("fsdp", None),
            P("fsdp", None),
            P("fsdp"),
            P("fsdp", None),
            P("fsdp", None),
        ),
        check_vma=False,
    )
```

time: 448 us -> 344 us (0.77)
  blocking collectives: 40.2 us -> 0 us
  waiting for transfers between devices: 177 us -> 138 us
  starting transfers between devices: 107 us -> 77.5 us
    ppermute x24 -> x30, waiting for transfers between devices: 76.6 us -> 23.7 us  [swap(): return lax.ppermute(array, 'fsdp', [(i, i ^ mask) for i in range(4)])]
    psum x1 -> x0, blocking collectives: 40.2 us -> none  [on_device(): lax.psum(jnp.stack([grad_gain_one[0], grad_gain_two]), ('ctx', 'fsdp'))]
    ppermute x84 -> x56, starting transfers between devices: 92.9 us -> 62.1 us  [shift(): return lax.ppermute(array, 'ctx', pairs)]
    ppermute x84 -> x56, waiting for transfers between devices: 100 us -> 115 us  [shift(): return lax.ppermute(array, 'ctx', pairs)]
    convert_element_type x10 -> x22, other arithmetic: 3.06 us -> 14.9 us  [the longest x14 10.1 us: add_all(): sum((part.astype(f32) for part in group)).astype(bf16)]
    select_n x4, other arithmetic: 9.46 us -> 1.62 us  [in_order(): first = [jnp.where(high, b, a) for a, b in zip(low_pair, high_pair)]]
    pallas_call x5 -> x9, Pallas kernels: 58.8 us -> 63.8 us  [the longest x2 31 us: attend_back(): pl.pallas_call(partial(attend_back_kernel, groups, per, base, before is n...]
    unnamed x153 -> x275, local copies, waits for them, and re-layouts: 8.15 us -> 11.5 us
  transfers between devices with their start and end apart: 108 -> 86, of which waited for: 48 -> 44; matrix products, arithmetic and copies ran while one was open for 7% -> 8% of each run, Pallas kernels for 3% -> 15%
where the time goes in v2:
time: 344 us; the launch traced here: 339 us
  waiting for transfers between devices  138 us (40%)
  starting transfers between devices  77.5 us (23%)
  Pallas kernels  67.5 us (20%)
  other arithmetic  28.7 us (8%)
  local copies, waits for them, and re-layouts  14 us (4%)
  matrix products  10.1 us (3%)
    ppermute x56, waiting for transfers between devices, shift(): return lax.ppermute(array, 'ctx', pairs)  115 us
    ppermute x56, starting transfers between devices, shift(): return lax.ppermute(array, 'ctx', pairs)  62.1 us
    pallas_call x2, Pallas kernels, attend_back(): pl.pallas_call(partial(attend_back_kernel, groups, per, base, before is n...  31 us
    ppermute x30, waiting for transfers between devices, swap(): return lax.ppermute(array, 'fsdp', [(i, i ^ mask) for i in range(4)])  23.7 us
    pallas_call x2, Pallas kernels, attend(): pl.pallas_call(partial(attend_kernel, groups, per, base, bool(before)), g...  17.6 us
    ppermute x30, starting transfers between devices, swap(): return lax.ppermute(array, 'fsdp', [(i, i ^ mask) for i in range(4)])  15.4 us
    unnamed x275, local copies, waits for them, and re-layouts  11.5 us
    convert_element_type x14, other arithmetic, add_all(): sum((part.astype(f32) for part in group)).astype(bf16)  10.1 us
  transfers between devices with their start and end apart: 86, of which 44 were waited for; matrix products, arithmetic and copies ran while one was open for 8% of the time, Pallas kernels for 15%

profile of v2, /device:TPU:0, one launch (start us, length us, event | category | flops | bytes accessed | tf_op | source)
XLA Modules:
  0.0 338.9 jit_solution(17105206200615339591)
XLA Ops:
  5.1 8.1 %collective-permute-done.1.w2.k2 = bf16[208,768]{1,0:T(8,128)(2,1)S(1)} collective-permute-done((bf16[208,768]{1,0:T(8,128)(2,1)S(1)}, bf16[208,768]{1,0:T(8,128)(2,1)S(1)}, u32[]{:S(2)}, u32[]{:S(2)}) %collective-permute-start.1) | collective-permute-done | bytes 319520 | tf_op jit(solution)/shard_map/ppermute | solution.py:145
  16.6 5.4 %collective-permute-done.3.w2.v2 = bf16[192,768]{1,0:T(8,128)(2,1)S(1)} collective-permute-done((bf16[192,768]{1,0:T(8,128)(2,1)S(1)}, bf16[192,768]{1,0:T(8,128)(2,1)S(1)}, u32[]{:S(2)}, u32[]{:S(2)}) %collective-permute-start.3) | collective-permute-done | bytes 294944 | tf_op jit(solution)/shard_map/ppermute | solution.py:145
  43.1 3.9 %collective-permute-done.19 = bf16[256,768]{1,0:T(8,128)(2,1)} collective-permute-done((bf16[256,768]{1,0:T(8,128)(2,1)S(1)}, bf16[256,768]{1,0:T(8,128)(2,1)}, u32[]{:S(2)}, u32[]{:S(2)}) %collective-permute-start.19) | collective-permute-done | bytes 393248 | tf_op jit(solution)/shard_map/ppermute | solution.py:54
  53.7 6.8 %collective-permute-done.8 = bf16[256,768]{1,0:T(8,128)(2,1)} collective-permute-done((bf16[256,768]{1,0:T(8,128)(2,1)}, bf16[256,768]{1,0:T(8,128)(2,1)}, u32[]{:S(2)}, u32[]{:S(2)}) %collective-permute-start.8) | collective-permute-done | bytes 393248 | tf_op jit(solution)/shard_map/ppermute | solution.py:54
  71.5 5.9 %collective-permute-done.9 = bf16[256,768]{1,0:T(8,128)(2,1)} collective-permute-done((bf16[256,768]{1,0:T(8,128)(2,1)}, bf16[256,768]{1,0:T(8,128)(2,1)}, u32[]{:S(2)}, u32[]{:S(2)}) %collective-permute-start.9) | collective-permute-done | bytes 393248 | tf_op jit(solution)/shard_map/ppermute | solution.py:54
  79.6 9.3 %attend_0.1 = (f32[256,768]{1,0:T(8,128)}, f32[256,768]{1,0:T(8,128)}, f32[256,768]{1,0:T(8,128)}, f32[256,768]{1,0:T(8,128)}) custom-call(s32[8]{0:T(128)} %copy-done.87, bf16[256,768]{1,0:T(8,128)(2,1)} %copy-done.49, bf16[1,256,768]{2,1,0:T(8,128)(2,1)} %bitcast.69, bf16[1,256,768]{2,1,0:T(8,128)(2,1)} %bitcast.11.refs_1_, bf16[1,256,768]{2,1,0:T(8,128)(2,1)} %bitcast.79, ...), custom_call_target="tpu_custom_call" | custom-call | flops 11500000256 | bytes 1000 | tf_op jit(solution)/shard_map/attend_0/pallas_call | solution.py:445
  91.1 8.3 %attend_5.1 = (bf16[256,768]{1,0:T(8,128)(2,1)}, f32[256,768]{1,0:T(8,128)}, f32[256,768]{1,0:T(8,128)}) custom-call(s32[8]{0:T(128)} %copy-done.87, bf16[256,768]{1,0:T(8,128)(2,1)} %copy-done.49, bf16[1,256,768]{2,1,0:T(8,128)(2,1)} %bitcast.4.refs_0_.refs_2_, bf16[1,256,768]{2,1,0:T(8,128)(2,1)} %bitcast.85, bf16[1,256,768]{2,1,0:T(8,128)(2,1)} %bitcast.6.refs_2_.refs_4_, ...), custom_call_target="tpu_custom_call" | custom-call | flops 6899999744 | bytes 1000 | tf_op jit(solution)/shard_map/attend_5/pallas_call | solution.py:445
  112.1 17.5 %attend_back_3.1 = (f32[256,768]{1,0:T(8,128)}, bf16[1,256,768]{2,1,0:T(8,128)(2,1)}, bf16[1,256,768]{2,1,0:T(8,128)(2,1)}, bf16[1,256,768]{2,1,0:T(8,128)(2,1)}...) custom-call(s32[8]{0:T(128)} %copy-done.87, ...), custom_call_target="tpu_custom_call" | custom-call | flops 25874999296 | bytes 1000 | tf_op jit(solution)/shard_map/attend_back_3/pallas_call | solution.py:554
  152.0 6.1 %collective-permute-done.34 = bf16[256,768]{1,0:T(8,128)(2,1)} collective-permute-done((bf16[256,768]{1,0:T(8,128)(2,1)}, bf16[256,768]{1,0:T(8,128)(2,1)}, u32[]{:S(2)}, u32[]{:S(2)}) %collective-permute-start.34) | collective-permute-done | bytes 393248 | tf_op jit(solution)/shard_map/ppermute | solution.py:54
  158.1 13.5 %attend_back_0.1 = (bf16[256,768]{1,0:T(8,128)(2,1)}, bf16[1,256,768]{2,1,0:T(8,128)(2,1)}, bf16[1,256,768]{2,1,0:T(8,128)(2,1)}, bf16[1,256,768]{2,1,0:T(8,128)...) custom-call(s32[8]{0:T(128)} %copy-done.87, ...), custom_call_target="tpu_custom_call" | custom-call | flops 15525000192 | bytes 1000 | tf_op jit(solution)/shard_map/attend_back_0/pallas_call | solution.py:554
  185.9 6.9 %collective-permute-done.43 = bf16[256,768]{1,0:T(8,128)(2,1)S(1)} collective-permute-done((bf16[256,768]{1,0:T(8,128)(2,1)S(1)}, bf16[256,768]{1,0:T(8,128)(2,1)S(1)}, u32[]{:S(2)}, u32[]{:S(2)}) %collective-permute-start.43) | collective-permute-done | bytes 393248 | tf_op jit(solution)/shard_map/ppermute | solution.py:54
  192.8 4.7 %collective-permute-done.45 = bf16[256,768]{1,0:T(8,128)(2,1)S(1)} collective-permute-done((bf16[256,768]{1,0:T(8,128)(2,1)S(1)}, bf16[256,768]{1,0:T(8,128)(2,1)S(1)}, u32[]{:S(2)}, u32[]{:S(2)}) %collective-permute-start.45) | collective-permute-done | bytes 393248 | tf_op jit(solution)/shard_map/ppermute | solution.py:54
  197.5 4.2 %collective-permute-done.46 = bf16[192,2304]{1,0:T(8,128)(2,1)S(1)} collective-permute-done((bf16[192,2304]{1,0:T(8,128)(2,1)S(1)}, bf16[192,2304]{1,0:T(8,128)(2,1)S(1)}, u32[]{:S(2)}, u32[]{:S(2)}) %collective-permute-start.46) | collective-permute-done | bytes 884768 | tf_op jit(solution)/shard_map/ppermute | solution.py:145
  208.3 5.7 %collective-permute-done.47.k_one = bf16[256,768]{1,0:T(8,128)(2,1)S(1)} collective-permute-done((bf16[256,768]{1,0:T(8,128)(2,1)S(1)}, bf16[256,768]{1,0:T(8,128)(2,1)S(1)}, u32[]{:S(2)}, u32[]{:S(2)}) %collective-permute-start.47) | collective-permute-done | bytes 393248 | tf_op jit(solution)/shard_map/ppermute | solution.py:54
  214.0 5.9 %collective-permute-done.48.v_one = bf16[256,768]{1,0:T(8,128)(2,1)S(1)} collective-permute-done((bf16[256,768]{1,0:T(8,128)(2,1)S(1)}, bf16[256,768]{1,0:T(8,128)(2,1)S(1)}, u32[]{:S(2)}, u32[]{:S(2)}) %collective-permute-start.48) | collective-permute-done | bytes 393248 | tf_op jit(solution)/shard_map/ppermute | solution.py:54
  219.8 5.2 %collective-permute-done.50.v_two = bf16[256,768]{1,0:T(8,128)(2,1)S(1)} collective-permute-done((bf16[256,768]{1,0:T(8,128)(2,1)S(1)}, bf16[256,768]{1,0:T(8,128)(2,1)S(1)}, u32[]{:S(2)}, u32[]{:S(2)}) %collective-permute-start.50) | collective-permute-done | bytes 393248 | tf_op jit(solution)/shard_map/ppermute | solution.py:54
  227.4 7.8 %kv_back.1 = (bf16[192,1792]{1,0:T(8,128)(2,1)S(1)}, bf16[192,1792]{1,0:T(8,128)(2,1)}, bf16[192,1792]{1,0:T(8,128)(2,1)S(1)}, bf16[192,1792]{1,0:T(8,128)(2,1)S(1)}, f32[256,768]{1,0:T(8,128)}) custom-call(s32[1]{0:T(128)} %bitcast.1.me, bf16[4,256,192]{2,1,0:T(8,128)(2,1)S(1)} %copy-done.48, bf16[256,768]{1,0:T(8,128)(2,1)S(1)} %bitcast.73, ...), custom_call_target="tpu_custom_call" | custom-call | flops 9200000000 | bytes 1000 | tf_op jit(solution)/shard_map/kv_back/pallas_call | solution.py:723
  241.0 5.9 %collective-permute-done.57 = bf16[24,5120]{1,0:T(8,128)(2,1)S(1)} collective-permute-done((bf16[24,5120]{1,0:T(8,128)(2,1)S(1)}, bf16[24,5120]{1,0:T(8,128)(2,1)S(1)}, u32[]{:S(2)}, u32[]{:S(2)}) %collective-permute-start.57) | collective-permute-done | bytes 245792 | tf_op jit(solution)/shard_map/ppermute | solution.py:54
  258.3 4.2 %collective-permute-done.60 = bf16[24,5120]{1,0:T(8,128)(2,1)S(1)} collective-permute-done((bf16[24,5120]{1,0:T(8,128)(2,1)S(1)}, bf16[24,5120]{1,0:T(8,128)(2,1)S(1)}, u32[]{:S(2)}, u32[]{:S(2)}) %collective-permute-start.60) | collective-permute-done | bytes 245792 | tf_op jit(solution)/shard_map/ppermute | solution.py:54
  283.2 3.8 %collective-permute-done.67 = bf16[24,1792]{1,0:T(8,128)(2,1)S(1)} collective-permute-done((bf16[24,1792]{1,0:T(8,128)(2,1)S(1)}, bf16[24,1792]{1,0:T(8,128)(2,1)S(1)}, u32[]{:S(2)}, u32[]{:S(2)}) %collective-permute-start.67) | collective-permute-done | bytes 86048 | tf_op jit(solution)/shard_map/ppermute | solution.py:54
  292.9 4.6 %collective-permute-done.72 = bf16[24,5120]{1,0:T(8,128)(2,1)S(1)} collective-permute-done((bf16[24,5120]{1,0:T(8,128)(2,1)S(1)}, bf16[24,5120]{1,0:T(8,128)(2,1)S(1)}, u32[]{:S(2)}, u32[]{:S(2)}) %collective-permute-start.72) | collective-permute-done | bytes 245792 | tf_op jit(solution)/shard_map/ppermute | solution.py:54
  304.6 4.6 %collective-permute-done.76 = bf16[24,5120]{1,0:T(8,128)(2,1)S(1)} collective-permute-done((bf16[24,5120]{1,0:T(8,128)(2,1)S(1)}, bf16[24,5120]{1,0:T(8,128)(2,1)S(1)}, u32[]{:S(2)}, u32[]{:S(2)}) %collective-permute-start.76) | collective-permute-done | bytes 245792 | tf_op jit(solution)/shard_map/ppermute | solution.py:54
  314.5 3.8 %collective-permute-done.80 = bf16[24,5120]{1,0:T(8,128)(2,1)S(1)} collective-permute-done((bf16[24,5120]{1,0:T(8,128)(2,1)S(1)}, bf16[24,5120]{1,0:T(8,128)(2,1)S(1)}, u32[]{:S(2)}, u32[]{:S(2)}) %collective-permute-start.80) | collective-permute-done | bytes 245792 | tf_op jit(solution)/shard_map/ppermute | solution.py:54
  331.9 4.2 %collective-permute-done.85 = bf16[24,1792]{1,0:T(8,128)(2,1)S(1)} collective-permute-done((bf16[24,1792]{1,0:T(8,128)(2,1)S(1)}, bf16[24,1792]{1,0:T(8,128)(2,1)S(1)}, u32[]{:S(2)}, u32[]{:S(2)}) %collective-permute-start.85) | collective-permute-done | bytes 86048 | tf_op jit(solution)/shard_map/ppermute | solution.py:54
  (514 shorter events, 179.5 us)
Async XLA Ops:
  29.6 17.4 %collective-permute-start.19 = (bf16[256,768]{1,0:T(8,128)(2,1)S(1)}, bf16[256,768]{1,0:T(8,128)(2,1)}, u32[]{:S(2)}, u32[]{:S(2)}) collective-permute-start(bf16[256,768]{1,0:T(8,128)(2,1)S(1)} %project_values.1), channel_id=1, source_target_pairs={{0,4},{8,0},{16,8},{24,16},{28,24},{20,28},{12,20},{4,12},{1,5},{9... | collective-permute-start | bytes 1179656 | tf_op jit(solution)/shard_map/ppermute | solution.py:54
  41.6 19.0 %collective-permute-start.8 = (bf16[256,768]{1,0:T(8,128)(2,1)}, bf16[256,768]{1,0:T(8,128)(2,1)}, u32[]{:S(2)}, u32[]{:S(2)}) collective-permute-start(bf16[256,768]{1,0:T(8,128)(2,1)} %collective-permute-done.7), channel_id=1, source_target_pairs={{0,8},{8,16},{16,24},{24,28},{28,20},{20,12},{12,4},{4,0},{1,9},{9... | collective-permute-start | bytes 1179656 | tf_op jit(solution)/shard_map/ppermute | solution.py:54
  47.0 15.1 %collective-permute-start.20 = (bf16[256,768]{1,0:T(8,128)(2,1)}, bf16[256,768]{1,0:T(8,128)(2,1)}, u32[]{:S(2)}, u32[]{:S(2)}) collective-permute-start(bf16[256,768]{1,0:T(8,128)(2,1)} %collective-permute-done.19), channel_id=1, source_target_pairs={{0,4},{8,0},{16,8},{24,16},{28,24},{20,28},{12,20},{4,12},{1,5},{9... | collective-permute-start | bytes 1179656 | tf_op jit(solution)/shard_map/ppermute | solution.py:54
  47.5 20.2 %collective-permute-start.11 = (bf16[256,768]{1,0:T(8,128)(2,1)}, bf16[256,768]{1,0:T(8,128)(2,1)S(1)}, u32[]{:S(2)}, u32[]{:S(2)}) collective-permute-start(bf16[256,768]{1,0:T(8,128)(2,1)} %copy-done.81), channel_id=1, source_target_pairs={{0,4},{8,0},{16,8},{24,16},{28,24},{20,28},{12,20},{4,12},{1,5},{9... | collective-permute-start | bytes 1179656 | tf_op jit(solution)/shard_map/ppermute | solution.py:54
  49.1 19.2 %collective-permute-start.24 = (bf16[192,768]{1,0:T(8,128)(2,1)S(1)}, bf16[192,768]{1,0:T(8,128)(2,1)S(1)}, u32[]{:S(2)}, u32[]{:S(2)}) collective-permute-start(bf16[192,768]{1,0:T(8,128)(2,1)S(1)} %collective-permute-done.23), channel_id=1, source_target_pairs={{0,1},{1,0},{2,3},{3,2},{4,5},{5,4},{6,7},{7,6},{8,9},{9,8},{10,11... | collective-permute-start | bytes 884744 | tf_op jit(solution)/shard_map/ppermute | solution.py:145
  52.1 17.7 %collective-permute-start.17 = (bf16[256,768]{1,0:T(8,128)(2,1)}, bf16[256,768]{1,0:T(8,128)(2,1)S(1)}, u32[]{:S(2)}, u32[]{:S(2)}) collective-permute-start(bf16[256,768]{1,0:T(8,128)(2,1)} %collective-permute-done.16), channel_id=1, source_target_pairs={{0,8},{8,16},{16,24},{24,28},{28,20},{20,12},{12,4},{4,0},{1,9},{9... | collective-permute-start | bytes 1179656 | tf_op jit(solution)/shard_map/ppermute | solution.py:54
  60.6 16.9 %collective-permute-start.9 = (bf16[256,768]{1,0:T(8,128)(2,1)}, bf16[256,768]{1,0:T(8,128)(2,1)}, u32[]{:S(2)}, u32[]{:S(2)}) collective-permute-start(bf16[256,768]{1,0:T(8,128)(2,1)} %collective-permute-done.8), channel_id=1, source_target_pairs={{0,8},{8,16},{16,24},{24,28},{28,20},{20,12},{12,4},{4,0},{1,9},{9... | collective-permute-start | bytes 1179656 | tf_op jit(solution)/shard_map/ppermute | solution.py:54
  62.1 16.9 %collective-permute-start.21 = (bf16[256,768]{1,0:T(8,128)(2,1)}, bf16[256,768]{1,0:T(8,128)(2,1)}, u32[]{:S(2)}, u32[]{:S(2)}) collective-permute-start(bf16[256,768]{1,0:T(8,128)(2,1)} %collective-permute-done.20), channel_id=1, source_target_pairs={{0,4},{8,0},{16,8},{24,16},{28,24},{20,28},{12,20},{4,12},{1,5},{9... | collective-permute-start | bytes 1179656 | tf_op jit(solution)/shard_map/ppermute | solution.py:54
  67.7 21.2 %collective-permute-start.26 = (bf16[192,2304]{1,0:T(8,128)(2,1)S(1)}, bf16[192,2304]{1,0:T(8,128)(2,1)S(1)}, u32[]{:S(2)}, u32[]{:S(2)}) collective-permute-start(bf16[192,2304]{1,0:T(8,128)(2,1)S(1)} %copy-done.54), channel_id=1, source_target_pairs={{0,2},{1,3},{2,0},{3,1},{4,6},{5,7},{6,4},{7,5},{8,10},{9,11},{10,... | collective-permute-start | bytes 2654216 | tf_op jit(solution)/shard_map/ppermute | solution.py:145
  68.2 20.8 %collective-permute-start.12 = (bf16[256,768]{1,0:T(8,128)(2,1)S(1)}, bf16[256,768]{1,0:T(8,128)(2,1)S(1)}, u32[]{:S(2)}, u32[]{:S(2)}) collective-permute-start(bf16[256,768]{1,0:T(8,128)(2,1)S(1)} %collective-permute-done.11), channel_id=1, source_target_pairs={{0,4},{8,0},{16,8},{24,16},{28,24},{20,28},{12,20},{4,12},{1,5},{9... | collective-permute-start | bytes 1179656 | tf_op jit(solution)/shard_map/ppermute | solution.py:54
  69.8 19.8 %collective-permute-start.18 = (bf16[256,768]{1,0:T(8,128)(2,1)S(1)}, bf16[256,768]{1,0:T(8,128)(2,1)S(1)}, u32[]{:S(2)}, u32[]{:S(2)}) collective-permute-start(bf16[256,768]{1,0:T(8,128)(2,1)S(1)} %collective-permute-done.17), channel_id=1, source_target_pairs={{0,8},{8,16},{16,24},{24,28},{28,20},{20,12},{12,4},{4,0},{1,9},{9... | collective-permute-start | bytes 1179656 | tf_op jit(solution)/shard_map/ppermute | solution.py:54
  131.7 18.7 %collective-permute-start.35 = (bf16[256,768]{1,0:T(8,128)(2,1)}, bf16[256,768]{1,0:T(8,128)(2,1)}, u32[]{:S(2)}, u32[]{:S(2)}) collective-permute-start(bf16[256,768]{1,0:T(8,128)(2,1)} %bitcast.90), channel_id=1, source_target_pairs={{0,4},{8,0},{16,8},{24,16},{28,24},{20,28},{12,20},{4,12},{1,5},{9... | collective-permute-start | bytes 1179656 | tf_op jit(solution)/shard_map/ppermute | solution.py:54
  133.3 18.7 %collective-permute-start.36 = (bf16[256,768]{1,0:T(8,128)(2,1)}, bf16[256,768]{1,0:T(8,128)(2,1)}, u32[]{:S(2)}, u32[]{:S(2)}) collective-permute-start(bf16[256,768]{1,0:T(8,128)(2,1)} %bitcast.89), channel_id=1, source_target_pairs={{0,8},{8,16},{16,24},{24,28},{28,20},{20,12},{12,4},{4,0},{1,9},{9... | collective-permute-start | bytes 1179656 | tf_op jit(solution)/shard_map/ppermute | solution.py:54
  148.0 23.6 %collective-permute-start.37 = (bf16[256,768]{1,0:T(8,128)(2,1)}, bf16[256,768]{1,0:T(8,128)(2,1)}, u32[]{:S(2)}, u32[]{:S(2)}) collective-permute-start(bf16[256,768]{1,0:T(8,128)(2,1)} %fusion.13), channel_id=1, source_target_pairs={{0,8},{8,16},{16,24},{24,28},{28,20},{20,12},{12,4},{4,0},{1,9},{9... | collective-permute-start | bytes 1179656 | tf_op jit(solution)/shard_map/ppermute | solution.py:54
  148.5 23.1 %collective-permute-start.38 = (bf16[192,2304]{1,0:T(8,128)(2,1)}, bf16[192,2304]{1,0:T(8,128)(2,1)S(1)}, u32[]{:S(2)}, u32[]{:S(2)}) collective-permute-start(bf16[192,2304]{1,0:T(8,128)(2,1)} %copy-done.22), channel_id=1, source_target_pairs={{0,1},{1,0},{2,3},{3,2},{4,5},{5,4},{6,7},{7,6},{8,9},{9,8},{10,11... | collective-permute-start | bytes 2654216 | tf_op jit(solution)/shard_map/ppermute | solution.py:145
  150.4 21.3 %collective-permute-start.39 = (bf16[192,2304]{1,0:T(8,128)(2,1)S(1)}, bf16[192,2304]{1,0:T(8,128)(2,1)S(1)}, u32[]{:S(2)}, u32[]{:S(2)}) collective-permute-start(bf16[192,2304]{1,0:T(8,128)(2,1)S(1)} %copy-done.21), channel_id=1, source_target_pairs={{0,1},{1,0},{2,3},{3,2},{4,5},{5,4},{6,7},{7,6},{8,9},{9,8},{10,11... | collective-permute-start | bytes 2654216 | tf_op jit(solution)/shard_map/ppermute | solution.py:145
  152.0 19.6 %collective-permute-start.40 = (bf16[192,2048]{1,0:T(8,128)(2,1)}, bf16[192,2048]{1,0:T(8,128)(2,1)S(1)}, u32[]{:S(2)}, u32[]{:S(2)}) collective-permute-start(bf16[192,2048]{1,0:T(8,128)(2,1)} %copy-done.24), channel_id=1, source_target_pairs={{0,1},{1,0},{2,3},{3,2},{4,5},{5,4},{6,7},{7,6},{8,9},{9,8},{10,11... | collective-permute-start | bytes 2359304 | tf_op jit(solution)/shard_map/ppermute | solution.py:145
  175.4 17.4 %collective-permute-start.43 = (bf16[256,768]{1,0:T(8,128)(2,1)S(1)}, bf16[256,768]{1,0:T(8,128)(2,1)S(1)}, u32[]{:S(2)}, u32[]{:S(2)}) collective-permute-start(bf16[256,768]{1,0:T(8,128)(2,1)S(1)} %fusion.11), channel_id=1, source_target_pairs={{0,4},{8,0},{16,8},{24,16},{28,24},{20,28},{12,20},{4,12},{1,5},{9... | collective-permute-start | bytes 1179656 | tf_op jit(solution)/shard_map/ppermute | solution.py:54
  179.8 17.8 %collective-permute-start.45 = (bf16[256,768]{1,0:T(8,128)(2,1)S(1)}, bf16[256,768]{1,0:T(8,128)(2,1)S(1)}, u32[]{:S(2)}, u32[]{:S(2)}) collective-permute-start(bf16[256,768]{1,0:T(8,128)(2,1)S(1)} %fusion.9), channel_id=1, source_target_pairs={{0,8},{8,16},{16,24},{24,28},{28,20},{20,12},{12,4},{4,0},{1,9},{9... | collective-permute-start | bytes 1179656 | tf_op jit(solution)/shard_map/ppermute | solution.py:54
  180.7 21.0 %collective-permute-start.46 = (bf16[192,2304]{1,0:T(8,128)(2,1)S(1)}, bf16[192,2304]{1,0:T(8,128)(2,1)S(1)}, u32[]{:S(2)}, u32[]{:S(2)}) collective-permute-start(bf16[192,2304]{1,0:T(8,128)(2,1)S(1)} %add_convert_fusion.1), channel_id=1, source_target_pairs={{0,2},{1,3},{2,0},{3,1},{4,6},{5,7},{6,4},{7,5},{8,10},{9,11},{10,... | collective-permute-start | bytes 2654216 | tf_op jit(solution)/shard_map/ppermute | solution.py:145
  203.4 16.4 %collective-permute-start.48 = (bf16[256,768]{1,0:T(8,128)(2,1)S(1)}, bf16[256,768]{1,0:T(8,128)(2,1)S(1)}, u32[]{:S(2)}, u32[]{:S(2)}) collective-permute-start(bf16[256,768]{1,0:T(8,128)(2,1)S(1)} %add_convert_fusion.9), channel_id=1, source_target_pairs={{0,4},{8,0},{16,8},{24,16},{28,24},{20,28},{12,20},{4,12},{1,5},{9... | collective-permute-start | bytes 1179656 | tf_op jit(solution)/shard_map/ppermute | solution.py:54
  206.5 18.5 %collective-permute-start.50 = (bf16[256,768]{1,0:T(8,128)(2,1)S(1)}, bf16[256,768]{1,0:T(8,128)(2,1)S(1)}, u32[]{:S(2)}, u32[]{:S(2)}) collective-permute-start(bf16[256,768]{1,0:T(8,128)(2,1)S(1)} %add_convert_fusion.7), channel_id=1, source_target_pairs={{0,8},{8,16},{16,24},{24,28},{28,20},{20,12},{12,4},{4,0},{1,9},{9... | collective-permute-start | bytes 1179656 | tf_op jit(solution)/shard_map/ppermute | solution.py:54
  207.3 19.2 %collective-permute-start.51 = (bf16[192,2048]{1,0:T(8,128)(2,1)S(1)}, bf16[192,2048]{1,0:T(8,128)(2,1)S(1)}, u32[]{:S(2)}, u32[]{:S(2)}) collective-permute-start(bf16[192,2048]{1,0:T(8,128)(2,1)S(1)} %add_convert_fusion.3), channel_id=1, source_target_pairs={{0,2},{1,3},{2,0},{3,1},{4,6},{5,7},{6,4},{7,5},{8,10},{9,11},{10,... | collective-permute-start | bytes 2359304 | tf_op jit(solution)/shard_map/ppermute | solution.py:145
  250.7 16.4 %collective-permute-start.58 = (bf16[192,1792]{1,0:T(8,128)(2,1)S(1)}, bf16[192,1792]{1,0:T(8,128)(2,1)S(1)}, u32[]{:S(2)}, u32[]{:S(2)}) collective-permute-start(bf16[192,1792]{1,0:T(8,128)(2,1)S(1)} %add_convert_fusion.5), channel_id=1, source_target_pairs={{0,2},{1,3},{2,0},{3,1},{4,6},{5,7},{6,4},{7,5},{8,10},{9,11},{10,... | collective-permute-start | bytes 2064392 | tf_op jit(solution)/shard_map/ppermute | solution.py:145
  (152 other events, 1603.0 us)
